TPU v7x, 128 devices: a whole 4x4x4 slice. The times are simulated.
128 devices in a mesh: gx: 16 (over z, y), gy: 8 (over x, core).
Axes of the slice: x: 4, y: 4, z: 4, core: 2. Of those that a mesh axis runs over, the one named last changes fastest.
Arguments:
- states: float32 [8, 64, 64, 1024], P(None, None, 'gx', 'gy'), may hold values from -6 to 6
- swept_volume: float32 [4, 64, 1024], P(None, 'gx', 'gy'), may hold values from -3 to 3
- flux_own: float32 [4, 64, 64], replicated, may hold values from -0.75 to 0.75
- flux_next: float32 [4, 64, 64], replicated, may hold values from -0.75 to 0.75
- mass_inverse: float32 [64, 64], replicated, may hold values from -0.75 to 0.75
- projection: float32 [4, 64, 64], replicated, may hold values from -0.75 to 0.75
- new_owner: int32 [16, 8, 512, 4], P('gx', 'gy'), may hold values from 0 to 127, all different within a row; in each aligned block of 512 rows (0 to 511, 512 to 1023, ..., all dimensions but the last counted through in order) at most 32 rows name the same one
- new_slot: int32 [16, 8, 512, 4], P('gx', 'gy'), may hold values from 0 to 511
- intersection_weight: float32 [16, 8, 512, 4], P('gx', 'gy'), may hold values from 0.2 to 1
Outputs:
- remapped: float32 [8, 64, 65536], P(None, None, ('gx', 'gy'))
Inputs may be any that keep to these rules, and one draw needn't show every extreme that they name: `new_owner`: each old element names 4 different owners; among the 512 old elements of one device no owner is named more than 32 times, a bound that some block reaches.
All inputs are finite; a program needn't handle non-finite values.
Results may differ from a plain program's by a relative error of at most 0.0003.
Values sent between devices are 32-bit elements; how exact they have to be, the bound alone decides.
A program may use at most 128 MiB of HBM per device.

v0:
```python
import jax
import jax.numpy as jnp
from jax import lax
from jax.sharding import PartitionSpec as P

PRECISE = lax.Precision.HIGHEST
MARGIN = 0.75


def with_halo(cells, sides, width):
    for axis, dim in sides:
        count = lax.axis_size(axis)
        ends = count - 1
        head = lax.slice_in_dim(cells, 0, width, axis=dim)
        tail = lax.slice_in_dim(cells, cells.shape[dim] - width, cells.shape[dim], axis=dim)
        cells = jnp.concatenate(
            [
                lax.ppermute(tail, axis, [(i, (i + 1) % count) for i in range(ends)]),
                cells,
                lax.ppermute(head, axis, [((i + 1) % count, i) for i in range(ends)]),
            ],
            axis=dim,
        )
    return cells


def nodal_product(matrix, values):
    return jnp.einsum("pq,fqxy->fpxy", matrix, values, precision=PRECISE)


def advance(padded, volumes, flux_own, flux_next, mass_inverse):
    center = padded[:, :, 1:-1, 1:-1]
    beside = (
        padded[:, :, :-2, 1:-1],
        padded[:, :, 2:, 1:-1],
        padded[:, :, 1:-1, :-2],
        padded[:, :, 1:-1, 2:],
    )
    summed = jnp.zeros(center.shape, jnp.float32)
    for side_index in range(4):
        outward = jnp.maximum(volumes[side_index], 0.0)
        inward = jnp.minimum(volumes[side_index], 0.0)
        summed = (
            summed
            + outward * nodal_product(flux_own[side_index], center)
            + inward * nodal_product(flux_next[side_index], beside[side_index])
        )
    return center - nodal_product(mass_inverse, summed)


def limit_nodes(advanced, padded_means):
    center = padded_means[:, 1:-1, 1:-1]
    neighbours = (
        padded_means[:, :-2, 1:-1],
        padded_means[:, 2:, 1:-1],
        padded_means[:, 1:-1, :-2],
        padded_means[:, 1:-1, 2:],
    )
    lower_bound = center
    upper_bound = center
    for neighbour in neighbours:
        lower_bound = jnp.minimum(lower_bound, neighbour)
        upper_bound = jnp.maximum(upper_bound, neighbour)
    return jnp.clip(advanced, (lower_bound - MARGIN)[:, None], (upper_bound + MARGIN)[:, None])


def fix_edges(padded_means, cell_means):
    first_x = lax.axis_index("gx") == 0
    last_x = lax.axis_index("gx") == lax.axis_size("gx") - 1
    first_y = lax.axis_index("gy") == 0
    last_y = lax.axis_index("gy") == lax.axis_size("gy") - 1
    padded_means = padded_means.at[:, 0, 1:-1].set(
        jnp.where(first_x, cell_means[:, 0, :], padded_means[:, 0, 1:-1])
    )
    padded_means = padded_means.at[:, -1, 1:-1].set(
        jnp.where(last_x, cell_means[:, -1, :], padded_means[:, -1, 1:-1])
    )
    padded_means = padded_means.at[:, 1:-1, 0].set(
        jnp.where(first_y, cell_means[:, :, 0], padded_means[:, 1:-1, 0])
    )
    padded_means = padded_means.at[:, 1:-1, -1].set(
        jnp.where(last_y, cell_means[:, :, -1], padded_means[:, 1:-1, -1])
    )
    return padded_means


def body(
    states,
    swept_volume,
    flux_own,
    flux_next,
    mass_inverse,
    projection,
    new_owner,
    new_slot,
    intersection_weight,
):
    fields, node_count, rows_x, rows_y = states.shape
    padded = with_halo(states, (("gx", 2), ("gy", 3)), 1)
    advanced = advance(padded, swept_volume, flux_own, flux_next, mass_inverse)
    cell_means = jnp.mean(advanced, axis=1)
    padded_means = with_halo(cell_means, (("gx", 1), ("gy", 2)), 1)
    padded_means = fix_edges(padded_means, cell_means)
    limited = limit_nodes(advanced, padded_means)
    old_count = rows_x * rows_y
    slots_each = new_owner.shape[-1]
    grid_x = lax.axis_size("gx")
    grid_y = lax.axis_size("gy")
    devices = grid_x * grid_y
    capacity = 2 * old_count * slots_each // devices
    width_all = fields * node_count
    flat_state = limited.reshape(fields, node_count, old_count)
    weights = intersection_weight.reshape(old_count, slots_each)
    projected = (
        jnp.einsum("kpq,fqe->ekfp", projection, flat_state, precision=PRECISE)
        * weights[:, :, None, None]
    )
    blocks = projected.reshape(old_count * slots_each, width_all)
    owners = new_owner.reshape(-1)
    onehot = (owners[:, None] == jnp.arange(devices, dtype=jnp.int32)[None, :]).astype(jnp.int32)
    ranking = jnp.sum((jnp.cumsum(onehot, axis=0) - 1) * onehot, axis=1)
    position = owners * capacity + ranking
    outgoing = jnp.zeros((devices * capacity, width_all), jnp.float32).at[position].set(blocks)
    places = (
        jnp.zeros((devices * capacity,), jnp.float32)
        .at[position]
        .set(new_slot.reshape(-1).astype(jnp.float32))
    )
    incoming, arrived = (
        lax.all_to_all(outgoing, ("gx", "gy"), split_axis=0, concat_axis=0, tiled=True),
        lax.all_to_all(places, ("gx", "gy"), split_axis=0, concat_axis=0, tiled=True),
    )
    summed = (
        jnp.zeros((old_count, width_all), jnp.float32).at[arrived.astype(jnp.int32)].add(incoming)
    )
    return jnp.einsum(
        "pq,nfq->fpn",
        mass_inverse,
        summed.reshape(old_count, fields, node_count),
        precision=PRECISE,
    )


def solution(mesh):
    placed = (
        P(None, None, "gx", "gy"),
        P(None, "gx", "gy"),
        P(),
        P(),
        P(),
        P(),
        P("gx", "gy", None, None),
        P("gx", "gy", None, None),
        P("gx", "gy", None, None),
    )
    return jax.shard_map(
        body, mesh=mesh, in_specs=placed, out_specs=P(None, None, ("gx", "gy")), check_vma=False
    )
```

profile of v0, /device:TPU:0, one launch (start us, length us, event | category | flops | bytes accessed | tf_op | source)
XLA Modules:
  0.0 272.0 jit_solution(175201953587795213)
XLA Ops:
  2.5 3.6 %collective-permute-start = (f32[8,64,1,128]{3,1,2,0:T(8,128)S(1)}, f32[8,64,1,128]{3,1,2,0:T(8,128)S(1)}, u32[]{:S(2)}, u32[]{:S(2)}) collective-permute-start(f32[8,64,1,128]{3,1,2,0:T(8,128)S(1)} %get-tuple-element.56), channel_id=1, source_target_pairs={{0,8},{8,16},{16,24},{24,32},{32,40},{40,48},{48,56},{56,64},{64,7... | collective-permute-start | bytes 786440 | tf_op jit(solution)/shard_map/ppermute | solution.py:18
  9.1 2.1 convolution_multiply_fusion.5
  11.2 2.1 convolution_multiply_fusion.6
  16.1 2.9 %convolution_multiply_fusion.7 = f32[8,4,128,64]{2,3,1,0:T(8,128)} fusion(f32[4,128]{1,0:T(4,128)} %get-tuple-element.68, f32[4,64,64]{2,1,0:T(8,128)} %param.19, f32[8,64,4,128]{3,2,1,0:T(4,128)S(1)} %copy-done.1), kind=kOutput, calls=%fused_computation.19 | convolution fusion | flops 201588736 | bytes 2131968 | tf_op jit(solution)/shard_map/pq,fqxy->fpxy/dot_general | solution.py:28
  19.2 2.2 fusion.55
  28.3 3.2 %convolution_multiply_fusion = f32[8,4,128,64]{2,3,1,0:T(8,128)} fusion(f32[8,64,1,128]{3,1,2,0:T(8,128)S(1)} %collective-permute-done.1, f32[8,64,4,128]{3,1,2,0:T(8,128)} %copy-done.2, f32[4,128]{1,0:T(4,128)S(1)} %copy-done.20, f32[4,64,64]{2,1,0:T(8,128)S(1)} %copy-done.8), kind=kOutput, calls=%fused_computation.6 | convolution fusion | flops 201916416 | bytes 2394112 | tf_op jit(solution)/shard_map/pq,fqxy->fpxy/dot_general | solution.py:28
  33.2 2.7 convolution_multiply_fusion.4
  36.0 2.7 fusion.10
  38.6 2.9 %fusion.5 = f32[8,4,128,64]{2,3,1,0:T(8,128)} fusion(f32[8,4,128,64]{2,3,1,0:T(8,128)S(1)} %fusion.10, f32[4,128]{1,0:T(4,128)S(1)} %copy-done.19, f32[4,64,64]{2,1,0:T(8,128)} %param.19, f32[8,64,4,128]{3,2,1,0:T(4,128)S(1)} %copy-done.1), kind=kOutput, calls=%fused_computation.15 | convolution fusion | flops 201850880 | bytes 3180544 | tf_op jit(solution)/shard_map/pq,fqxy->fpxy/dot_general | solution.py:28
  43.2 3.1 %fusion.4 = f32[8,64,4,128]{3,1,2,0:T(8,128)S(1)} fusion(f32[8,4,128,64]{2,3,1,0:T(8,128)} %fusion.5, f32[8,64,6,1]{3,1,2,0:T(8,128)} %copy.59, f32[8,64,6,128]{3,1,2,0:T(8,128)S(1)} %constant_dynamic-update-slice_fusion, f32[4,128]{1,0:T(4,128)S(1)} %copy-done.14, f32[4,64,64]{2,1,0:T(8,128)S(1)} %copy-done.8), kind=kOutput, calls=%fused_computation.13 | convolution fusion | flops 202113024 | bytes 3717120 | tf_op jit(solution)/shard_map/pq,fqxy->fpxy/dot_general | solution.py:28
  47.5 4.4 %collective-permute-start.4 = (f32[8,1,128]{2,1,0:T(1,128)S(1)}, f32[8,1,128]{2,1,0:T(1,128)S(1)}, u32[]{:S(2)}, u32[]{:S(2)}) collective-permute-start(f32[8,1,128]{2,1,0:T(1,128)S(1)} %slice.270), channel_id=1, source_target_pairs={{0,8},{8,16},{16,24},{24,32},{32,40},{40,48},{48,56},{56,64},{64,7... | collective-permute-start | bytes 12296 | tf_op jit(solution)/shard_map/ppermute | solution.py:18
  52.3 8.1 %scatter_custom_fusion = f32[4096]{0:T(1024)S(1)} fusion(s32[2048]{0:T(1024)S(1)} %bitcast.133, f32[2048]{0:T(1024)S(1)} %reshape.291, f32[]{:T(128)} %constant.149.clone.1), kind=kCustom, calls=%fused_computation.80 | custom fusion | bytes 16388 | tf_op jit(solution)/shard_map/scatter | solution.py:127
  61.0 15.5 %all-to-all-start = ((f32[128,32,1]{1,2,0:T(1,128)}), f32[128,32,1]{1,2,0:T(1,128)S(1)}, u32[]{:S(2)}, u32[]{:S(2)}) async-start(f32[128,32,1]{1,2,0:T(1,128)} %bitcast.5), calls=%async_computation | async-start | bytes 131072 | tf_op jit(solution)/shard_map/all_to_all | solution.py:131
  78.6 3.5 %collective-permute-done.5 = f32[8,1,128]{2,1,0:T(1,128)S(1)} collective-permute-done((f32[8,1,128]{2,1,0:T(1,128)S(1)}, f32[8,1,128]{2,1,0:T(1,128)S(1)}, u32[]{:S(2)}, u32[]{:S(2)}) %collective-permute-start.5) | collective-permute-done | bytes 4128 | tf_op jit(solution)/shard_map/ppermute | solution.py:20
  85.0 2.8 %collective-permute-done.7 = f32[8,6,1]{2,1,0:T(8,128)S(1)} collective-permute-done((f32[8,6,1]{2,1,0:T(8,128)S(1)}, f32[8,6,1]{2,1,0:T(8,128)S(1)}, u32[]{:S(2)}, u32[]{:S(2)}) %collective-permute-start.7) | collective-permute-done | bytes 224 | tf_op jit(solution)/shard_map/ppermute | solution.py:20
  87.9 2.6 scatter.29
  95.5 4.9 %multiply_bitcast_fusion = f32[512,4,8,64]{0,3,1,2:T(8,128)} fusion(f32[512,4]{0,1:T(4,128)S(1)} %bitcast.132, f32[8,64,512,1]{2,1,0,3:T(8,128)S(1)} %reshape.320, f32[4,64,64]{2,1,0:T(8,128)S(1)} %copy-done), kind=kOutput, calls=%fused_computation.3 | convolution fusion | flops 806354944 | bytes 5316608 | tf_op jit(solution)/shard_map/kpq,fqe->ekfp/dot_general | solution.py:115
  100.4 9.1 %copy.62 = f32[512,4,8,64]{3,2,1,0:T(8,128)} copy(f32[512,4,8,64]{0,3,1,2:T(8,128)} %multiply_bitcast_fusion) | data formatting | bytes 8388608 | tf_op jit(solution)/shard_map/mul | solution.py:115
  109.6 7.5 %reshape.299 = f32[2048,512]{1,0:T(8,128)} reshape(f32[512,4,8,64]{3,2,1,0:T(8,128)} %copy.62) | data formatting | bytes 8388608 | tf_op jit(solution)/shard_map/reshape | solution.py:118
  117.0 13.4 %scatter_custom_fusion.1 = f32[4096,512]{1,0:T(8,128)} fusion(s32[2048]{0:T(1024)S(1)} %bitcast.134, f32[2048,512]{1,0:T(8,128)} %reshape.299, f32[]{:T(128)} %constant.149.clone.1), kind=kCustom, calls=%fused_computation.4 | custom fusion | bytes 8389120 | tf_op jit(solution)/shard_map/scatter | solution.py:123
  130.4 14.9 %all-to-all-start.1 = ((f32[128,32,512]{2,1,0:T(8,128)}), f32[128,32,512]{2,1,0:T(8,128)}, u32[]{:S(2)}, u32[]{:S(2)}) async-start(f32[128,32,512]{2,1,0:T(8,128)} %bitcast.128), calls=%async_computation.1 | async-start | bytes 16777216 | tf_op jit(solution)/shard_map/all_to_all | solution.py:130
  145.7 97.9 %all-to-all-done.1 = f32[128,32,512]{2,1,0:T(8,128)} async-done(((f32[128,32,512]{2,1,0:T(8,128)}), f32[128,32,512]{2,1,0:T(8,128)}, u32[]{:S(2)}, u32[]{:S(2)}) %all-to-all-start.1) | async-done | bytes 8388640 | tf_op jit(solution)/shard_map/all_to_all | solution.py:130
  243.5 26.1 %scatter_custom_fusion.2 = f32[512,512]{1,0:T(8,128)S(1)} fusion(s32[4096]{0:T(1024)S(1)} %bitcast.131, f32[4096,512]{1,0:T(8,128)} %bitcast.50, f32[]{:T(128)} %constant.149.clone.1), kind=kCustom, calls=%fused_computation.45 | custom fusion | flops 2097152 | bytes 1049088 | tf_op jit(solution)/shard_map/scatter-add | solution.py:134
  269.9 2.1 convolution_bitcast_fusion
  (107 shorter events, 31.4 us)
Async XLA Ops:
  0.0 95.2 %copy-start = (f32[4,64,64]{2,1,0:T(8,128)S(1)}, f32[4,64,64]{2,1,0:T(8,128)}, u32[]{:S(2)}) copy-start(f32[4,64,64]{2,1,0:T(8,128)} %param.22) | copy-start | bytes 196612
  0.0 9.1 %copy-start.1 = (f32[8,64,4,128]{3,2,1,0:T(4,128)S(1)}, f32[8,64,4,128]{3,2,1,0:T(4,128)}, u32[]{:S(2)}) copy-start(f32[8,64,4,128]{3,2,1,0:T(4,128)} %param.17) | copy-start | bytes 3145732
  0.0 7.4 %copy-start.11 = (s32[1,1,512,4]{2,3,1,0:T(4,128)S(1)}, s32[1,1,512,4]{2,3,1,0:T(4,128)}, u32[]{:S(2)}) copy-start(s32[1,1,512,4]{2,3,1,0:T(4,128)} %param.23) | copy-start | bytes 24580
  0.0 8.5 %copy-start.17 = (f32[4,4,128]{2,1,0:T(4,128)S(1)}, f32[4,4,128]{2,1,0:T(4,128)}, u32[]{:S(2)}) copy-start(f32[4,4,128]{2,1,0:T(4,128)} %param.18) | copy-start | bytes 24580
  0.0 9.1 %copy-start.7 = (f32[4,64,64]{2,1,0:T(8,128)S(1)}, f32[4,64,64]{2,1,0:T(8,128)}, u32[]{:S(2)}) copy-start(f32[4,64,64]{2,1,0:T(8,128)} %param.19) | copy-start | bytes 196612
  2.5 16.4 %collective-permute-start = (f32[8,64,1,128]{3,1,2,0:T(8,128)S(1)}, f32[8,64,1,128]{3,1,2,0:T(8,128)S(1)}, u32[]{:S(2)}, u32[]{:S(2)}) collective-permute-start(f32[8,64,1,128]{3,1,2,0:T(8,128)S(1)} %get-tuple-element.56), channel_id=1, source_target_pairs={{0,8},{8,16},{16,24},{24,32},{32,40},{40,48},{48,56},{56,64},{64,7... | collective-permute-start | bytes 786440 | tf_op jit(solution)/shard_map/ppermute | solution.py:18
  6.1 13.0 %collective-permute-start.1 = (f32[8,64,1,128]{3,1,2,0:T(8,128)S(1)}, f32[8,64,1,128]{3,1,2,0:T(8,128)S(1)}, u32[]{:S(2)}, u32[]{:S(2)}) collective-permute-start(f32[8,64,1,128]{3,1,2,0:T(8,128)S(1)} %get-tuple-element.55), channel_id=1, source_target_pairs={{8,0},{16,8},{24,16},{32,24},{40,32},{48,40},{56,48},{64,56},{72,6... | collective-permute-start | bytes 786440 | tf_op jit(solution)/shard_map/ppermute | solution.py:20
  21.4 6.9 %copy-start.8 = (f32[4,64,64]{2,1,0:T(8,128)S(1)}, f32[4,64,64]{2,1,0:T(8,128)}, u32[]{:S(2)}) copy-start(f32[4,64,64]{2,1,0:T(8,128)} %param.20) | copy-start | bytes 196612
  21.4 6.9 %copy-start.20 = (f32[4,128]{1,0:T(4,128)S(1)}, f32[4,128]{1,0:T(4,128)}, u32[]{:S(2)}) copy-start(f32[4,128]{1,0:T(4,128)} %get-tuple-element.65) | copy-start | bytes 6148
  23.3 8.1 %collective-permute-start.2 = (f32[8,64,6,1]{1,0,3,2:T(8,128)S(1)}, f32[8,64,6,1]{1,0,3,2:T(8,128)S(1)}, u32[]{:S(2)}, u32[]{:S(2)}) collective-permute-start(f32[8,64,6,1]{1,0,3,2:T(8,128)S(1)} %copy.55), channel_id=1, source_target_pairs={{0,1},{1,2},{2,3},{3,4},{4,5},{5,6},{6,7},{8,9},{9,10},{10,11},{11... | collective-permute-start | bytes 36872 | tf_op jit(solution)/shard_map/ppermute | solution.py:18
  26.7 14.8 %collective-permute-start.3 = (f32[8,64,6,1]{1,0,3,2:T(8,128)S(1)}, f32[8,64,6,1]{1,0,3,2:T(8,128)S(1)}, u32[]{:S(2)}, u32[]{:S(2)}) collective-permute-start(f32[8,64,6,1]{1,0,3,2:T(8,128)S(1)} %copy.58), channel_id=1, source_target_pairs={{1,0},{2,1},{3,2},{4,3},{5,4},{6,5},{7,6},{9,8},{10,9},{11,10},{12... | collective-permute-start | bytes 36872 | tf_op jit(solution)/shard_map/ppermute | solution.py:20
  28.3 4.9 %copy-start.16 = (f32[4,128]{1,0:T(4,128)S(1)}, f32[4,128]{1,0:T(4,128)}, u32[]{:S(2)}) copy-start(f32[4,128]{1,0:T(4,128)} %get-tuple-element.66) | copy-start | bytes 6148
  33.2 2.7 copy-start.5
  33.2 2.7 copy-start.6
  33.2 2.7 copy-start.15
  43.2 3.1 %copy-start.9 = (f32[64,64]{1,0:T(8,128)S(1)}, f32[64,64]{1,0:T(8,128)}, u32[]{:S(2)}) copy-start(f32[64,64]{1,0:T(8,128)} %param.21) | copy-start | bytes 49156
  46.3 5.6 %copy-start.10 = (s32[2048,1]{0,1:T(1,128)S(1)}, s32[2048,1]{0,1:T(1,128)}, u32[]{:S(2)}) copy-start(s32[2048,1]{0,1:T(1,128)} %mul.114) | copy-start | bytes 24580
  46.3 5.6 %copy-start.18 = (s32[1,1,512,4]{2,3,1,0:T(4,128)S(1)}, s32[1,1,512,4]{2,3,1,0:T(4,128)}, u32[]{:S(2)}) copy-start(s32[1,1,512,4]{2,3,1,0:T(4,128)} %param.24) | copy-start | bytes 24580
  47.5 29.1 %collective-permute-start.4 = (f32[8,1,128]{2,1,0:T(1,128)S(1)}, f32[8,1,128]{2,1,0:T(1,128)S(1)}, u32[]{:S(2)}, u32[]{:S(2)}) collective-permute-start(f32[8,1,128]{2,1,0:T(1,128)S(1)} %slice.270), channel_id=1, source_target_pairs={{0,8},{8,16},{16,24},{24,32},{32,40},{40,48},{48,56},{56,64},{64,7... | collective-permute-start | bytes 12296 | tf_op jit(solution)/shard_map/ppermute | solution.py:18
  61.0 69.4 %all-to-all-start = ((f32[128,32,1]{1,2,0:T(1,128)}), f32[128,32,1]{1,2,0:T(1,128)S(1)}, u32[]{:S(2)}, u32[]{:S(2)}) async-start(f32[128,32,1]{1,2,0:T(1,128)} %bitcast.5), calls=%async_computation | async-start | bytes 131072 | tf_op jit(solution)/shard_map/all_to_all | solution.py:131
  76.6 5.5 %collective-permute-start.5 = (f32[8,1,128]{2,1,0:T(1,128)S(1)}, f32[8,1,128]{2,1,0:T(1,128)S(1)}, u32[]{:S(2)}, u32[]{:S(2)}) collective-permute-start(f32[8,1,128]{2,1,0:T(1,128)S(1)} %get-tuple-element.62), channel_id=1, source_target_pairs={{8,0},{16,8},{24,16},{32,24},{40,32},{48,40},{56,48},{64,56},{72,6... | collective-permute-start | bytes 12296 | tf_op jit(solution)/shard_map/ppermute | solution.py:20
  82.2 2.8 %collective-permute-start.6 = (f32[8,6,1]{2,1,0:T(8,128)S(1)}, f32[8,6,1]{2,1,0:T(8,128)S(1)}, u32[]{:S(2)}, u32[]{:S(2)}) collective-permute-start(f32[8,6,1]{2,1,0:T(8,128)S(1)} %get-tuple-element.59), channel_id=1, source_target_pairs={{0,1},{1,2},{2,3},{3,4},{4,5},{5,6},{6,7},{8,9},{9,10},{10,11},{11... | collective-permute-start | bytes 584 | tf_op jit(solution)/shard_map/ppermute | solution.py:18
  83.5 4.3 %collective-permute-start.7 = (f32[8,6,1]{2,1,0:T(8,128)S(1)}, f32[8,6,1]{2,1,0:T(8,128)S(1)}, u32[]{:S(2)}, u32[]{:S(2)}) collective-permute-start(f32[8,6,1]{2,1,0:T(8,128)S(1)} %get-tuple-element.60), channel_id=1, source_target_pairs={{1,0},{2,1},{3,2},{4,3},{5,4},{6,5},{7,6},{9,8},{10,9},{11,10},{12... | collective-permute-start | bytes 584 | tf_op jit(solution)/shard_map/ppermute | solution.py:20
  130.4 113.1 %all-to-all-start.1 = ((f32[128,32,512]{2,1,0:T(8,128)}), f32[128,32,512]{2,1,0:T(8,128)}, u32[]{:S(2)}, u32[]{:S(2)}) async-start(f32[128,32,512]{2,1,0:T(8,128)} %bitcast.128), calls=%async_computation.1 | async-start | bytes 16777216 | tf_op jit(solution)/shard_map/all_to_all | solution.py:130
  (7 other events, 12.2 us)
where the time goes:
time: 277 us; the launch traced here: 272 us
  waiting for transfers between devices  104 us (38%)
  local copies, waits for them, and re-layouts  61.7 us (22%)
  starting transfers between devices  46.7 us (17%)
  matrix products  29.6 us (11%)
  other arithmetic  29.2 us (11%)
    all_to_all x1, waiting for transfers between devices, body(): lax.all_to_all(outgoing, ('gx', 'gy'), split_axis=0, concat_axis=0, tiled...  97.9 us
    scatter-add x1, other arithmetic, body(): jnp.zeros((old_count, width_all), jnp.float32).at[arrived.astype(jnp.int32)]  26.1 us
    dot_general x9, matrix products, nodal_product(): return jnp.einsum('pq,fqxy->fpxy', matrix, values, precision=PRECISE)  22.6 us
    all_to_all x1, starting transfers between devices, body(): lax.all_to_all(places, ('gx', 'gy'), split_axis=0, concat_axis=0, tiled=T...  15.5 us
    all_to_all x1, starting transfers between devices, body(): lax.all_to_all(outgoing, ('gx', 'gy'), split_axis=0, concat_axis=0, tiled...  14.9 us
    scatter x1, local copies, waits for them, and re-layouts, body(): jnp.zeros((devices * capacity, width_all), jnp.float32).at[position]  13.4 us
    ppermute x4, starting transfers between devices, with_halo(): lax.ppermute(tail, axis, [(i, (i + 1) % count) for i in range(ends)])  10.7 us
    mul x1, local copies, waits for them, and re-layouts, body(): jnp.einsum('kpq,fqe->ekfp', projection, flat_state, precision=PRECISE)  9.13 us
  transfers between devices with their start and end apart: 10, of which 3 were waited for; matrix products, arithmetic and copies ran while one was open for 29% of the time, Pallas kernels for 0%

commit v1 on v0

v1 whole, which is shorter than its diff:
```python
import functools

import jax
import jax.numpy as jnp
from jax import lax
from jax.experimental import pallas as pl
from jax.experimental.pallas import tpu as pltpu
from jax.sharding import PartitionSpec as P

F, Q, K, EX, EY, CAP = 8, 64, 4, 4, 128, 32
E = EX * EY
COLS = F * Q
MARGIN = 0.75
MESH = pl.DeviceIdType.MESH
VMEM = pl.BlockSpec(memory_space=pltpu.VMEM)
F32, BF16 = jnp.float32, jnp.bfloat16
PARTS = ((0, 3, "xyz"), (3, 3, "yzx"), (6, 2, "zxy"))


def halves(values):
    high = values.astype(BF16)
    return high, (values - high.astype(F32)).astype(BF16)


def product(matrix, values):
    high, low = halves(values)
    stacked = jnp.concatenate([high, low, high], axis=0)
    return jnp.dot(matrix, stacked, preferred_element_type=F32)


def tables_kernel(rows_ref, inverse_ref, flux_ref, project_ref, table_ref, g_ref, p_ref):
    inverse = inverse_ref[...]
    for source, target, count in ((flux_ref, g_ref, 8), (project_ref, p_ref, 4)):
        for term in range(count):
            made = jnp.dot(
                inverse,
                source[term],
                precision=lax.Precision.HIGHEST,
                preferred_element_type=F32,
            )
            high, low = halves(made)
            target[term * Q : (term + 1) * Q, :] = jnp.concatenate([high, high, low], axis=1)
    devices = lax.broadcasted_iota(jnp.int32, (128, 256), 0).astype(F32)
    ranks = lax.broadcasted_iota(jnp.int32, (CAP, 256), 0).astype(F32)
    earlier = (
        lax.broadcasted_iota(jnp.int32, (256, 256), 0)
        < lax.broadcasted_iota(jnp.int32, (256, 256), 1)
    )
    earlier = jnp.where(earlier, 1.0, 0.0).astype(BF16)
    carry = jnp.zeros((128, 1), F32)
    table = jnp.zeros((128, 8 * CAP), F32)
    for chunk in range(E * K // 256):
        lanes = slice(chunk * 256, (chunk + 1) * 256)
        named = jnp.where(devices == rows_ref[0:1, lanes], 1.0, 0.0)
        before = jnp.dot(named.astype(BF16), earlier, preferred_element_type=F32) + carry
        rank = jnp.sum(named * before, axis=0, keepdims=True)
        carry = carry + jnp.sum(named, axis=1, keepdims=True)
        placed = ranks == rank
        weight = rows_ref[6:7, lanes]
        first = weight.astype(BF16).astype(F32)
        second = (weight - first).astype(BF16).astype(F32)
        parts = [rows_ref[1 + m : 2 + m, lanes] for m in range(5)]
        parts += [first, second, weight - first - second]
        values = jnp.concatenate([jnp.where(placed, row, 0.0) for row in parts], axis=0)
        table = table + lax.dot_general(
            named.astype(BF16),
            values.astype(BF16),
            (((1,), (1,)), ((), ())),
            preferred_element_type=F32,
        )
    table_ref[...] = table


def make_tables(new_owner, new_slot, weight, mass_inverse, flux, projection):
    owner = new_owner.reshape(E, K).T.reshape(E * K)
    slot = new_slot.reshape(E, K).T.reshape(E * K)
    weight = weight.reshape(E, K).T.reshape(E * K)
    which = jnp.arange(E * K, dtype=jnp.int32)
    element = which % E + 1
    rows = jnp.stack(
        [
            owner.astype(F32),
            (element // 128).astype(F32),
            (element % 128).astype(F32),
            (which // E).astype(F32),
            (slot // 128).astype(F32),
            (slot % 128).astype(F32),
            weight,
        ]
        + [jnp.zeros((E * K,), F32)]
    )
    table, g, p = pl.pallas_call(
        tables_kernel,
        out_shape=(
            jax.ShapeDtypeStruct((128, 8 * CAP), F32),
            jax.ShapeDtypeStruct((8 * Q, 3 * Q), BF16),
            jax.ShapeDtypeStruct((4 * Q, 3 * Q), BF16),
        ),
        in_specs=[VMEM] * 4,
        out_specs=[VMEM] * 3,
    )(rows, mass_inverse, flux, projection)
    t = table.reshape(4, 4, 4, 2, 8, CAP)
    full = jnp.stack(
        [
            t[..., 0, :] * 128 + t[..., 1, :] - 1,
            t[..., 2, :],
            t[..., 3, :] * 128 + t[..., 4, :],
            t[..., 5, :] + t[..., 6, :] + t[..., 7, :],
        ],
        axis=4,
    )
    full = jnp.pad(full, [(0, 0)] * 4 + [(0, 4), (0, 0)])
    spot = {"z": 0, "y": 1, "x": 2}
    made = []
    for _, _, (a, b, c) in PARTS:
        order = (spot[a], spot[b], 3, 4, spot[c], 5)
        made.append(jnp.transpose(full, order).reshape(4, 8, 8, 128))
    return made, g, p


def flux_kernel(
    u_ref, v_ref, g_ref, out_ref, sides, packed, means, mean_sides, mean_packed, bounds, send, recv
):
    gx, gy = lax.axis_index("gx"), lax.axis_index("gy")
    n_x, n_y = lax.axis_size("gx"), lax.axis_size("gy")
    near = (
        (lax.rem(gx + n_x - 1, n_x), gy),
        (lax.rem(gx + 1, n_x), gy),
        (gx, lax.rem(gy + n_y - 1, n_y)),
        (gx, lax.rem(gy + 1, n_y)),
    )
    inside = (gx > 0, gx < n_x - 1, gy > 0, gy < n_y - 1)
    barrier = pltpu.get_barrier_semaphore()
    for device in near:
        pl.semaphore_signal(barrier, inc=1, device_id=device, device_id_type=MESH)
    lane64 = lax.broadcasted_iota(jnp.int32, (Q, EY), 1)
    lane8 = lax.broadcasted_iota(jnp.int32, (8, EY), 1)
    field8 = lax.broadcasted_iota(jnp.int32, (8, EY), 0)

    def block(j):
        return slice(j * EY, (j + 1) * EY)

    def pack(f, _):
        rows = pl.ds(pl.multiple_of(f * Q, Q), Q)
        low = jnp.zeros((Q, EY), F32)
        high = jnp.zeros((Q, EY), F32)
        for j in range(EX):
            values = u_ref[rows, block(j)]
            low = jnp.where(lane64 == j, pltpu.roll(values, j, 1), low)
            high = jnp.where(lane64 == j, pltpu.roll(values, j + 1, 1), high)
        packed[0, rows, :] = low
        packed[1, rows, :] = high
        return 0

    lax.fori_loop(0, F, pack, 0)
    pl.semaphore_wait(barrier, 4)

    def exchange(sources, target, base):
        copies = []
        for s in range(4):
            copies.append(
                pltpu.make_async_remote_copy(
                    src_ref=sources[s],
                    dst_ref=target.at[s ^ 1],
                    send_sem=send.at[base + s],
                    recv_sem=recv.at[base + (s ^ 1)],
                    device_id=near[s],
                    device_id_type=MESH,
                )
            )
        for copy in copies:
            copy.start()
        return copies

    copies = exchange(
        (
            u_ref.at[:, pl.ds(0, EY)],
            u_ref.at[:, pl.ds(3 * EY, EY)],
            packed.at[0],
            packed.at[1],
        ),
        sides,
        0,
    )

    def interior(f, _):
        rows = pl.ds(pl.multiple_of(f * Q, Q), Q)
        u = u_ref[rows, :]
        made = product(g_ref[...], u)
        for j in range(EX):
            total = u[:, block(j)]
            for s in range(4):
                outward = jnp.maximum(v_ref[s : s + 1, block(j)], 0.0)
                total = total - outward * made[s * Q : (s + 1) * Q, block(j)]
            inward = [jnp.minimum(v_ref[s : s + 1, block(j)], 0.0) for s in range(4)]
            if j > 0:
                total = total - inward[0] * made[4 * Q : 5 * Q, block(j - 1)]
            if j < EX - 1:
                total = total - inward[1] * made[5 * Q : 6 * Q, block(j + 1)]
            before = pltpu.roll(made[6 * Q : 7 * Q, block(j)], 1, 1)
            after = pltpu.roll(made[7 * Q : 8 * Q, block(j)], EY - 1, 1)
            total = total - jnp.where(lane64 == 0, 0.0, inward[2] * before)
            total = total - jnp.where(lane64 == EY - 1, 0.0, inward[3] * after)
            out_ref[rows, block(j)] = total
        return 0

    lax.fori_loop(0, F, interior, 0)
    for copy in copies:
        copy.wait()
    gate = [jnp.where(here, 1.0, 0.0).astype(F32) for here in inside]

    def edges(f, found):
        found = list(found)
        rows = pl.ds(pl.multiple_of(f * Q, Q), Q)
        made = [
            product(g_ref[(4 + s) * Q : (5 + s) * Q, :], sides[s, rows, :]) for s in range(4)
        ]
        for j in range(EX):
            inward = [jnp.minimum(v_ref[s : s + 1, block(j)], 0.0) * gate[s] for s in range(4)]
            total = out_ref[rows, block(j)]
            if j == 0:
                total = total - inward[0] * made[0]
            if j == EX - 1:
                total = total - inward[1] * made[1]
            before = made[2] if j == 0 else pltpu.roll(made[2], EY - j, 1)
            after = pltpu.roll(made[3], EY - 1 - j, 1)
            total = total - jnp.where(lane64 == 0, inward[2] * before, 0.0)
            total = total - jnp.where(lane64 == EY - 1, inward[3] * after, 0.0)
            out_ref[rows, block(j)] = total
            mean = jnp.sum(total, axis=0, keepdims=True) * (1.0 / Q)
            found[j] = jnp.where(field8 == f, mean, found[j])
        return tuple(found)

    found = lax.fori_loop(0, F, edges, tuple(jnp.zeros((8, EY), F32) for _ in range(EX)))
    for j in range(EX):
        means[:, block(j)] = found[j]
    low = jnp.zeros((8, EY), F32)
    high = jnp.zeros((8, EY), F32)
    for j in range(EX):
        values = means[:, block(j)]
        low = jnp.where(lane8 == j, pltpu.roll(values, j, 1), low)
        high = jnp.where(lane8 == j, pltpu.roll(values, j + 1, 1), high)
    mean_packed[0] = low
    mean_packed[1] = high
    copies = exchange(
        (
            means.at[:, pl.ds(0, EY)],
            means.at[:, pl.ds(3 * EY, EY)],
            mean_packed.at[0],
            mean_packed.at[1],
        ),
        mean_sides,
        4,
    )
    for copy in copies:
        copy.wait()
    for j in range(EX):
        center = means[:, block(j)]
        left = means[:, block(j - 1)] if j > 0 else jnp.where(gate[0] > 0, mean_sides[0], center)
        right = (
            means[:, block(j + 1)] if j < EX - 1 else jnp.where(gate[1] > 0, mean_sides[1], center)
        )
        before = mean_sides[2] if j == 0 else pltpu.roll(mean_sides[2], EY - j, 1)
        before = jnp.where(gate[2] > 0, before, center)
        before = jnp.where(lane8 == 0, before, pltpu.roll(center, 1, 1))
        after = pltpu.roll(mean_sides[3], EY - 1 - j, 1)
        after = jnp.where(gate[3] > 0, after, center)
        after = jnp.where(lane8 == EY - 1, after, pltpu.roll(center, EY - 1, 1))
        lower, upper = center, center
        for other in (left, right, before, after):
            lower = jnp.minimum(lower, other)
            upper = jnp.maximum(upper, other)
        bounds[0, :, block(j)] = lower - MARGIN
        bounds[1, :, block(j)] = upper + MARGIN

    for f in range(F):
        rows = slice(f * Q, (f + 1) * Q)
        lower = bounds[0, f : f + 1, :]
        upper = bounds[1, f : f + 1, :]
        out_ref[rows, :] = jnp.minimum(jnp.maximum(out_ref[rows, :], lower), upper)


def advance_and_limit(states, volumes, g):
    return pl.pallas_call(
        flux_kernel,
        out_shape=jax.ShapeDtypeStruct((COLS, E), F32),
        in_specs=[VMEM] * 3,
        out_specs=VMEM,
        scratch_shapes=[
            pltpu.VMEM((4, COLS, EY), F32),
            pltpu.VMEM((2, COLS, EY), F32),
            pltpu.VMEM((8, E), F32),
            pltpu.VMEM((4, 8, EY), F32),
            pltpu.VMEM((2, 8, EY), F32),
            pltpu.VMEM((2, 8, E), F32),
            pltpu.SemaphoreType.DMA((8,)),
            pltpu.SemaphoreType.DMA((8,)),
        ],
        compiler_params=pltpu.CompilerParams(
            collective_id=0, has_side_effects=True, vmem_limit_bytes=24 * 2**20
        ),
    )(states, volumes, g)


def remap_kernel(
    lim_ref, t0, t1, t2, p_ref, out_ref,
    ar0, ar1, ar2, at0, at1, at2, bs0, bs1, bs2, br0, br1, br2,
    cs0, cs1, cs2, cr0, cr1, cr2, split, picked, pair,
    a_send, a_recv, t_send, t_recv, b_send, b_recv, c_send, c_recv, own_sem,
):
    tables, ar, at = (t0, t1, t2), (ar0, ar1, ar2), (at0, at1, at2)
    bs, br, cs, cr = (bs0, bs1, bs2), (br0, br1, br2), (cs0, cs1, cs2), (cr0, cr1, cr2)
    gx, gy = lax.axis_index("gx"), lax.axis_index("gy")
    here = {"x": gy // 2, "y": lax.rem(gx, 4), "z": gx // 4, "c": lax.rem(gy, 2)}

    def away(axis, distance, core=0):
        at_ = dict(here)
        at_[axis] = lax.rem(here[axis] + distance, 4)
        at_["c"] = lax.rem(here["c"] + core, 2)
        return (at_["z"] * 4 + at_["y"], at_["x"] * 2 + at_["c"])

    barrier = pltpu.get_barrier_semaphore()
    for axis in "xyz":
        for distance in (1, 2, 3):
            for core in (0, 1):
                pl.semaphore_signal(
                    barrier, inc=1, device_id=away(axis, distance, core), device_id_type=MESH
                )
    pl.semaphore_signal(barrier, inc=1, device_id=away("x", 0, 1), device_id_type=MESH)
    pl.semaphore_wait(barrier, 19)

    def states_copy(p, d):
        first, count, axes = PARTS[p]
        return pltpu.make_async_remote_copy(
            src_ref=lim_ref.at[pl.ds(first * Q, count * Q)],
            dst_ref=ar[p].at[3 - d],
            send_sem=a_send.at[p, d - 1],
            recv_sem=a_recv.at[p, d - 1],
            device_id=away(axes[0], d),
            device_id_type=MESH,
        )

    def table_copy(p, d):
        axis = PARTS[p][2][0]
        return pltpu.make_async_remote_copy(
            src_ref=tables[p].at[lax.rem(here[axis] + d, 4)],
            dst_ref=at[p].at[4 - d],
            send_sem=t_send.at[p, d - 1],
            recv_sem=t_recv.at[p, d - 1],
            device_id=away(axis, d),
            device_id_type=MESH,
        )

    def block_copy(p, d, core):
        axis = PARTS[p][2][1]
        return pltpu.make_async_remote_copy(
            src_ref=bs[p].at[d, lax.rem(here["c"] + core, 2)],
            dst_ref=br[p].at[lax.rem(4 - d, 4), :, :, pl.ds(core * 128, 128)],
            send_sem=b_send.at[p, d, core],
            recv_sem=b_recv.at[p, d, core],
            device_id=away(axis, d, core),
            device_id_type=MESH,
        )

    def own_copy(p):
        return pltpu.make_async_copy(
            bs[p].at[0, here["c"]], br[p].at[0, :, :, pl.ds(0, 128)], own_sem.at[p]
        )

    def sum_copy(p, d):
        axis = PARTS[p][2][2]
        return pltpu.make_async_remote_copy(
            src_ref=cs[p].at[lax.rem(here[axis] + d, 4)],
            dst_ref=cr[p].at[d - 1],
            send_sem=c_send.at[p, d - 1],
            recv_sem=c_recv.at[p, d - 1],
            device_id=away(axis, d),
            device_id_type=MESH,
        )

    for d in (2, 1, 3):
        for p in range(3):
            table_copy(p, d).start()
    for d in (2, 1, 3):
        for p in range(3):
            states_copy(p, d).start()

    element = lax.broadcasted_iota(jnp.int32, (E, 256), 0).astype(F32)
    quarter = lax.rem(lax.broadcasted_iota(jnp.int32, (1, 256), 1) // CAP, 4)

    def route(p):
        first, count, axes = PARTS[p]
        rows = count * Q
        me_a, me_b = here[axes[0]], here[axes[1]]
        at[p][0] = tables[p][me_a]
        for d in (0, 1, 3, 2):
            if d:
                states_copy(p, d).wait_recv()
                table_copy(p, d).wait_recv()
            j = (4 - d) % 4
            values = lim_ref[first * Q : first * Q + rows, :] if d == 0 else ar[p][3 - d]
            high, low = halves(values)
            split[j, 0:rows, :] = high
            split[j, rows : 2 * rows, :] = low

        def towards(step, _):
            d = 3 - step
            group = lax.rem(me_b + d, 4) * 2
            infos = []
            for j in range(4):
                info = jnp.concatenate(
                    [pltpu.roll(at[p][j, group + c], CAP * j, 1) if j else at[p][j, group + c] for c in range(2)],
                    axis=1,
                )
                infos.append(info)
                hot = jnp.where(element == info[0:1, :], 1.0, 0.0).astype(BF16)
                made = jnp.dot(split[j, 0 : 2 * rows, :], hot, preferred_element_type=F32)
                picked[j, 0:rows, :] = made[0:rows] + made[rows:]
            for o in range(4):
                info = infos[3]
                for j in range(3):
                    info = jnp.where(quarter == (o + j) % 4, infos[j], info)
                which, weight = info[1:2, :], info[3:4, :]
                for f in range(count):
                    part = slice(f * Q, (f + 1) * Q)
                    values = picked[3, part, :]
                    for j in range(3):
                        values = jnp.where(quarter == (o + j) % 4, picked[j, part, :], values)
                    made = product(p_ref[...], values)
                    chosen = made[3 * Q :]
                    for k in range(3):
                        chosen = jnp.where(which == float(k), made[k * Q : (k + 1) * Q], chosen)
                    chosen = chosen * weight
                    bs[p][d, 0, o, part, :] = chosen[:, 0:128]
                    bs[p][d, 1, o, part, :] = chosen[:, 128:256]
                bs[p][d, 0, o, rows : rows + 8, :] = info[:, 0:128]
                bs[p][d, 1, o, rows : rows + 8, :] = info[:, 128:256]
            block_copy(p, d, 1).start()

            @pl.when(d > 0)
            def _():
                block_copy(p, d, 0).start()

            return 0

        lax.fori_loop(0, 4, towards, 0)
        own_copy(p).start()

    def gather(p):
        _, count, axes = PARTS[p]
        rows = count * Q
        me_c = here[axes[2]]
        for number, d in enumerate((0, 1, 3, 2)):
            if d == 0:
                own_copy(p).wait()
                block_copy(p, 0, 1).wait_recv()
            else:
                block_copy(p, d, 0).wait_recv()
                block_copy(p, d, 1).wait_recv()
            slot_of = (4 - d) % 4

            def owner(step, _, number=number, slot_of=slot_of):
                distance = lax.rem(step + 2, 4)
                o = lax.rem(me_c + distance, 4)
                high, low = halves(br[p][slot_of, o, 0:rows, :])
                pair[0:rows, :] = high
                pair[rows : 2 * rows, :] = low
                hot = jnp.where(element == br[p][slot_of, o, rows + 2 : rows + 3, :], 1.0, 0.0)
                made = lax.dot_general(
                    pair[0 : 2 * rows, :],
                    hot.astype(BF16),
                    (((1,), (1,)), ((), ())),
                    preferred_element_type=F32,
                )
                total = made[0:rows] + made[rows:]
                if number > 0:
                    total = total + cs[p][o]
                cs[p][o] = total
                if number == 3:

                    @pl.when(distance > 0)
                    def _():
                        sum_copy(p, distance).start()

                return 0

            lax.fori_loop(0, 4, owner, 0)

    def finish(p):
        first, count, axes = PARTS[p]
        total = cs[p][here[axes[2]]]
        for d in (1, 3, 2):
            sum_copy(p, d).wait_recv()
            total = total + cr[p][d - 1]
        out_ref[first * Q : (first + count) * Q, :] = total

    for p in range(3):
        route(p)
    for p in (2, 0, 1):
        gather(p)
    for p in (2, 0, 1):
        finish(p)
    for p in range(3):
        for d in (1, 2, 3):
            states_copy(p, d).wait_send()
            table_copy(p, d).wait_send()
            block_copy(p, d, 0).wait_send()
            block_copy(p, d, 1).wait_send()
            sum_copy(p, d).wait_send()
        block_copy(p, 0, 1).wait_send()


def remap(limited, tables, p):
    rows = [count * Q for _, count, _ in PARTS]
    dma = pltpu.SemaphoreType.DMA
    return pl.pallas_call(
        remap_kernel,
        out_shape=jax.ShapeDtypeStruct((COLS, E), F32),
        in_specs=[VMEM] * 5,
        out_specs=VMEM,
        scratch_shapes=[pltpu.VMEM((3, r, E), F32) for r in rows]
        + [pltpu.VMEM((4, 8, 8, 128), F32) for r in rows]
        + [pltpu.VMEM((4, 2, 4, r + 8, 128), F32) for r in rows]
        + [pltpu.VMEM((4, 4, r + 8, 256), F32) for r in rows]
        + [pltpu.VMEM((4, r, E), F32) for r in rows]
        + [pltpu.VMEM((3, r, E), F32) for r in rows]
        + [
            pltpu.VMEM((4, 2 * max(rows), E), BF16),
            pltpu.VMEM((4, max(rows), 256), F32),
            pltpu.VMEM((2 * max(rows), 256), BF16),
            dma((3, 3)),
            dma((3, 3)),
            dma((3, 3)),
            dma((3, 3)),
            dma((3, 4, 2)),
            dma((3, 4, 2)),
            dma((3, 3)),
            dma((3, 3)),
            dma((3,)),
        ],
        compiler_params=pltpu.CompilerParams(
            collective_id=1, has_side_effects=True, vmem_limit_bytes=56 * 2**20
        ),
    )(limited, *tables, p)


def body(
    states,
    swept_volume,
    flux_own,
    flux_next,
    mass_inverse,
    projection,
    new_owner,
    new_slot,
    intersection_weight,
):
    flux = jnp.concatenate([flux_own, flux_next], axis=0)
    tables, g, p = make_tables(
        new_owner, new_slot, intersection_weight, mass_inverse, flux, projection
    )
    limited = advance_and_limit(states.reshape(COLS, E), swept_volume.reshape(4, E), g)
    return remap(limited, tables, p).reshape(F, Q, E)


def solution(mesh):
    placed = (
        P(None, None, "gx", "gy"),
        P(None, "gx", "gy"),
        P(),
        P(),
        P(),
        P(),
        P("gx", "gy", None, None),
        P("gx", "gy", None, None),
        P("gx", "gy", None, None),
    )
    return jax.shard_map(
        body, mesh=mesh, in_specs=placed, out_specs=P(None, None, ("gx", "gy")), check_vma=False
    )
```

time: 277 us -> 135 us (0.49); the launches traced: 272 us -> 134 us
  Pallas kernels: 0 us -> 122 us
  waiting for transfers between devices: 104 us -> 0 us
  local copies, waits for them, and re-layouts: 61.7 us -> 11.2 us
  starting transfers between devices: 46.7 us -> 0 us
  matrix products: 29.6 us -> 0 us
  other arithmetic: 29.2 us -> 1.3 us
    pallas_call x0 -> x3, Pallas kernels: none -> 122 us  [the longest x1 96 us: remap(): pl.pallas_call(remap_kernel, out_shape=jax.ShapeDtypeStruct((COLS, E), F3...]
    all_to_all x2 -> x0, waiting for transfers between devices: 97.9 us -> none  [the longest x1 97.9 us: body(): lax.all_to_all(outgoing, ('gx', 'gy'), split_axis=0, concat_axis=0, tiled...]
    all_to_all x2 -> x0, starting transfers between devices: 30.4 us -> none  [the longest x1 15.5 us: body(): lax.all_to_all(places, ('gx', 'gy'), split_axis=0, concat_axis=0, tiled=T...]
    dot_general x11 -> x0, matrix products: 29.6 us -> none  [the longest x9 22.6 us: nodal_product(): return jnp.einsum('pq,fqxy->fpxy', matrix, values, precision=PRECISE)]
    scatter x6 -> x0, local copies, waits for them, and re-layouts: 27.1 us -> none  [the longest x1 13.4 us: body(): jnp.zeros((devices * capacity, width_all), jnp.float32).at[position]]
    scatter-add x1 -> x0, other arithmetic: 26.1 us -> none  [body(): jnp.zeros((old_count, width_all), jnp.float32).at[arrived.astype(jnp.int32)]]
    ppermute x8 -> x0, starting transfers between devices: 16.3 us -> none  [the longest x4 10.7 us: with_halo(): lax.ppermute(tail, axis, [(i, (i + 1) % count) for i in range(ends)])]
    mul x3 -> x0, local copies, waits for them, and re-layouts: 10.1 us -> none  [the longest x1 9.13 us: body(): jnp.einsum('kpq,fqe->ekfp', projection, flat_state, precision=PRECISE)]
  transfers between devices with their start and end apart: 10 -> 0, of which waited for: 3 -> 0; matrix products, arithmetic and copies ran while one was open for 29% -> 0% of each run, Pallas kernels for 0% -> 0%
where the time goes in v1:
time: 135 us; the launch traced here: 134 us
  Pallas kernels  122 us (90%)
  local copies, waits for them, and re-layouts  11.2 us (8%)
    pallas_call x1, Pallas kernels, remap(): pl.pallas_call(remap_kernel, out_shape=jax.ShapeDtypeStruct((COLS, E), F3...  96 us
    pallas_call x1, Pallas kernels, advance_and_limit(): pl.pallas_call(flux_kernel, out_shape=jax.ShapeDtypeStruct((COLS, E), F32...  22.5 us
    unnamed x23, local copies, waits for them, and re-layouts  5.48 us
    pallas_call x1, Pallas kernels, make_tables(): pl.pallas_call(tables_kernel, out_shape=(jax.ShapeDtypeStruct((128, 8 * C...  3.2 us
    reshape x3, local copies, waits for them, and re-layouts, make_tables(): made.append(jnp.transpose(full, order).reshape(4, 8, 8, 128))  2.72 us

profile of v1, /device:TPU:0, one launch (start us, length us, event | category | flops | bytes accessed | tf_op | source)
XLA Modules:
  0.0 134.3 jit_solution(2914780777894143023)
XLA Ops:
  0.0 0.7 copy.31
  0.7 0.0 copy-start.5
  0.7 0.0 copy-start.6
  0.7 0.0 copy-start.3
  0.9 0.5 copy-done.5
  1.5 0.7 stack.4.rows_ref
  2.2 0.7 pad_maximum_fusion.flux_ref
  2.9 3.2 %shard_map.91 = (f32[128,256]{1,0:T(8,128)}, bf16[512,192]{1,0:T(8,128)(2,1)}, bf16[256,192]{1,0:T(8,128)(2,1)}) custom-call(f32[8,2048]{1,0:T(8,128)} %stack.4.rows_ref, f32[64,64]{1,0:T(8,128)} %inverse_ref.1, f32[8,64,64]{2,1,0:T(8,128)} %pad_maximum_fusion.flux_ref, f32[4,64,64]{2,1,0:T(8,128)} %project_ref.1), custom_call_target="tpu_custom_call" | custom-call | tf_op jit(solution)/shard_map/pallas_call | solution.py:92
  6.1 1.1 reshape.284
  7.2 0.5 fusion.10
  7.9 0.4 fusion.9
  8.2 0.3 copy.18
  8.6 0.9 reshape.285.t0
  9.5 0.3 copy.19
  9.8 0.9 reshape.286.t1
  10.7 0.9 reshape.287.t2
  11.6 0.1 copy.50
  11.7 0.6 copy-done.7
  12.3 0.3 copy-done.1
  12.6 22.5 %shard_map.92.lim_ref = f32[512,512]{1,0:T(8,128)S(1)} custom-call(f32[512,512]{1,0:T(8,128)S(1)} %bitcast.35, f32[4,512]{1,0:T(4,128)S(1)} %bitcast.36, bf16[512,192]{1,0:T(8,128)(2,1)S(1)} %copy-done.1), custom_call_target="tpu_custom_call" | custom-call | tf_op jit(solution)/shard_map/pallas_call | solution.py:284
  35.1 0.0 copy-start
  35.1 1.0 copy-done
  36.0 96.0 %shard_map.93 = f32[512,512]{1,0:T(8,128)} custom-call(f32[512,512]{1,0:T(8,128)} %copy-done, f32[4,8,8,128]{3,2,1,0:T(8,128)} %reshape.285.t0, f32[4,8,8,128]{3,2,1,0:T(8,128)} %reshape.286.t1, f32[4,8,8,128]{3,2,1,0:T(8,128)} %reshape.287.t2, bf16[256,192]{1,0:T(8,128)(2,1)} %get-tuple-element.10.p_ref), custom_call_target="tpu_custom_call" | custom-call | tf_op jit(solution)/shard_map/pallas_call | solution.py:516
  132.1 2.3 %copy.53 = f32[8,64,512]{2,1,0:T(8,128)} copy(f32[8,64,512]{2,1,0:T(8,128)} %bitcast.37) | data formatting | bytes 2097152
  (20 shorter events, 0.3 us)
Async XLA Ops:
  0.7 0.7 copy-start.5
  0.7 0.7 copy-start.6
  0.7 1.5 %copy-start.3 = (f32[4,64,64]{2,1,0:T(8,128)S(1)}, f32[4,64,64]{2,1,0:T(8,128)}, u32[]{:S(2)}) copy-start(f32[4,64,64]{2,1,0:T(8,128)} %param.12) | copy-start | bytes 196612
  0.7 1.5 %copy-start.4 = (f32[4,64,64]{2,1,0:T(8,128)S(1)}, f32[4,64,64]{2,1,0:T(8,128)}, u32[]{:S(2)}) copy-start(f32[4,64,64]{2,1,0:T(8,128)} %param.11) | copy-start | bytes 196612
  9.5 2.2 %copy-start.2 = (f32[8,64,4,128]{3,2,1,0:T(4,128)S(1)}, f32[8,64,4,128]{3,2,1,0:T(4,128)}, u32[]{:S(2)}) copy-start(f32[8,64,4,128]{3,2,1,0:T(4,128)} %param.9) | copy-start | bytes 3145732
  11.6 0.7 copy-start.7
  11.6 1.0 copy-start.1
  35.1 1.0 copy-start

commit v2 on v0

v2 whole, which is shorter than its diff:
```python
import functools

import jax
import jax.numpy as jnp
from jax import lax
from jax.experimental import pallas as pl
from jax.experimental.pallas import tpu as pltpu
from jax.sharding import PartitionSpec as P

F, Q, K, EX, EY, CAP = 8, 64, 4, 4, 128, 32
E = EX * EY
COLS = F * Q
MARGIN = 0.75
MESH = pl.DeviceIdType.MESH
VMEM = pl.BlockSpec(memory_space=pltpu.VMEM)
F32, BF16 = jnp.float32, jnp.bfloat16
PARTS = ((0, 3, "xyz"), (3, 3, "yzx"), (6, 2, "zxy"))


def halves(values):
    high = values.astype(BF16)
    return high, (values - high.astype(F32)).astype(BF16)


def product(matrix, values):
    high, low = halves(values)
    stacked = jnp.concatenate([high, low, high], axis=0)
    return jnp.dot(matrix, stacked, preferred_element_type=F32)


def fold(inverse_ref, sources, target_ref):
    inverse = inverse_ref[...]
    for term, source in enumerate(sources):
        made = jnp.dot(
            inverse, source, precision=lax.Precision.HIGHEST, preferred_element_type=F32
        )
        high, low = halves(made)
        target_ref[term * Q : (term + 1) * Q, :] = jnp.concatenate([high, high, low], axis=1)


def rank_table(rows_ref):
    devices = lax.broadcasted_iota(jnp.int32, (128, 256), 0).astype(F32)
    ranks = lax.broadcasted_iota(jnp.int32, (CAP, 256), 0).astype(F32)
    earlier = lax.broadcasted_iota(jnp.int32, (256, 256), 0) < lax.broadcasted_iota(
        jnp.int32, (256, 256), 1
    )
    earlier = jnp.where(earlier, 1.0, 0.0).astype(BF16)
    carry = jnp.zeros((128, 1), F32)
    table = jnp.zeros((128, 8 * CAP), F32)
    for chunk in range(E * K // 256):
        lanes = slice(chunk * 256, (chunk + 1) * 256)
        named = jnp.where(devices == rows_ref[0:1, lanes], 1.0, 0.0)
        before = jnp.dot(named.astype(BF16), earlier, preferred_element_type=F32) + carry
        rank = jnp.sum(named * before, axis=0, keepdims=True)
        carry = carry + jnp.sum(named, axis=1, keepdims=True)
        placed = ranks == rank
        weight = rows_ref[6:7, lanes]
        first = weight.astype(BF16).astype(F32)
        second = (weight - first).astype(BF16).astype(F32)
        parts = [rows_ref[1 + m : 2 + m, lanes] for m in range(5)]
        parts += [first, second, weight - first - second]
        values = jnp.concatenate([jnp.where(placed, row, 0.0) for row in parts], axis=0)
        table = table + lax.dot_general(
            named.astype(BF16),
            values.astype(BF16),
            (((1,), (1,)), ((), ())),
            preferred_element_type=F32,
        )
    return table.astype(BF16)


STRIDE = {"z": 32, "y": 8, "x": 2}


def part_table(table, axes, target_ref):
    a, b, c = axes
    row = lax.broadcasted_iota(jnp.int32, (32, 128), 0)
    lane = lax.broadcasted_iota(jnp.int32, (32, 128), 1)
    first = (row // 8) * STRIDE[a] + lax.rem(row // 2, 4) * STRIDE[b] + lax.rem(row, 2)
    quarter = lane // CAP
    made = [jnp.zeros((32, 128), F32)] * 8
    for o in range(4):
        chosen = jnp.where(lane == first + o * STRIDE[c], 1.0, 0.0).astype(BF16)
        found = jnp.dot(chosen, table, preferred_element_type=F32)
        for m in range(8):
            tile = found[:, (m // 4) * 128 : (m // 4 + 1) * 128]
            turn = (o - m % 4) % 4
            tile = pltpu.roll(tile, turn * CAP, 1) if turn else tile
            made[m] = jnp.where(quarter == o, tile, made[m])
    whats = (
        made[0] * 128 + made[1] - 1,
        made[2],
        made[3] * 128 + made[4],
        made[5] + made[6] + made[7],
    )
    for place in range(4):
        for number, what in enumerate(whats):
            target_ref[place, number] = what[place * 8 : (place + 1) * 8]


def kernel(
    u_ref, v_ref, inverse_ref, own_ref, next_ref, project_ref, rows_ref, out_ref,
    g_ref, p_ref, lim_ref, sides, packed, means, mean_sides, mean_packed,
    tb0, tb1, tb2, ar0, ar1, ar2, at0, at1, at2, bs0, bs1, bs2, br0, br1, br2,
    cs0, cs1, cs2, cr0, cr1, cr2, split, picked, pair,
    h_send, h_recv, m_send, m_recv,
    a_send, a_recv, t_send, t_recv, b_send, b_recv, c_send, c_recv, own_sem,
):
    tables, ar, at = (tb0, tb1, tb2), (ar0, ar1, ar2), (at0, at1, at2)
    bs, br, cs, cr = (bs0, bs1, bs2), (br0, br1, br2), (cs0, cs1, cs2), (cr0, cr1, cr2)
    gx, gy = lax.axis_index("gx"), lax.axis_index("gy")
    n_x, n_y = lax.axis_size("gx"), lax.axis_size("gy")
    here = {"x": gy // 2, "y": lax.rem(gx, 4), "z": gx // 4, "c": lax.rem(gy, 2)}
    near = (
        (lax.rem(gx + n_x - 1, n_x), gy),
        (lax.rem(gx + 1, n_x), gy),
        (gx, lax.rem(gy + n_y - 1, n_y)),
        (gx, lax.rem(gy + 1, n_y)),
    )
    inside = (gx > 0, gx < n_x - 1, gy > 0, gy < n_y - 1)
    gate = [jnp.where(there, 1.0, 0.0).astype(F32) for there in inside]

    def away(axis, distance, core=0):
        at_ = dict(here)
        at_[axis] = lax.rem(here[axis] + distance, 4)
        at_["c"] = lax.rem(here["c"] + core, 2)
        return (at_["z"] * 4 + at_["y"], at_["x"] * 2 + at_["c"])

    partners = [away(axis, d, core) for axis in "xyz" for d in (1, 2, 3) for core in (0, 1)]
    partners += [away("x", 0, 1), *near]
    barrier = pltpu.get_barrier_semaphore()
    for device in partners:
        pl.semaphore_signal(barrier, inc=1, device_id=device, device_id_type=MESH)

    def remote(source, target, send, recv, device):
        return pltpu.make_async_remote_copy(
            src_ref=source,
            dst_ref=target,
            send_sem=send,
            recv_sem=recv,
            device_id=device,
            device_id_type=MESH,
        )

    def rows_of(p):
        first, count, _ = PARTS[p]
        return pl.ds(first * Q, count * Q)

    def side_copy(p, s):
        rows = rows_of(p)
        source = (
            u_ref.at[rows, pl.ds(0, EY)],
            u_ref.at[rows, pl.ds(3 * EY, EY)],
            packed.at[0, rows],
            packed.at[1, rows],
        )[s]
        return remote(
            source, sides.at[s ^ 1, rows], h_send.at[p, s], h_recv.at[p, s ^ 1], near[s]
        )

    def mean_copy(p, s):
        source = (
            means.at[p, :, pl.ds(0, EY)],
            means.at[p, :, pl.ds(3 * EY, EY)],
            mean_packed.at[p, 0],
            mean_packed.at[p, 1],
        )[s]
        return remote(
            source, mean_sides.at[p, s ^ 1], m_send.at[p, s], m_recv.at[p, s ^ 1], near[s]
        )

    def states_copy(p, d):
        return remote(
            lim_ref.at[rows_of(p)],
            ar[p].at[3 - d],
            a_send.at[p, d - 1],
            a_recv.at[p, d - 1],
            away(PARTS[p][2][0], d),
        )

    def table_copy(p, d):
        axis = PARTS[p][2][0]
        return remote(
            tables[p].at[lax.rem(here[axis] + d, 4)],
            at[p].at[4 - d],
            t_send.at[p, d - 1],
            t_recv.at[p, d - 1],
            away(axis, d),
        )

    def block_copy(p, d, core):
        return remote(
            bs[p].at[d, lax.rem(here["c"] + core, 2)],
            br[p].at[lax.rem(4 - d, 4), :, :, pl.ds(core * 128, 128)],
            b_send.at[p, d, core],
            b_recv.at[p, d, core],
            away(PARTS[p][2][1], d, core),
        )

    def own_copy(p):
        return pltpu.make_async_copy(
            bs[p].at[0, here["c"]], br[p].at[0, :, :, pl.ds(0, 128)], own_sem.at[p]
        )

    def sum_copy(p, d):
        axis = PARTS[p][2][2]
        return remote(
            cs[p].at[lax.rem(here[axis] + d, 4)],
            cr[p].at[d - 1],
            c_send.at[p, d - 1],
            c_recv.at[p, d - 1],
            away(axis, d),
        )

    lane64 = lax.broadcasted_iota(jnp.int32, (Q, EY), 1)
    lane8 = lax.broadcasted_iota(jnp.int32, (8, EY), 1)
    row8 = lax.broadcasted_iota(jnp.int32, (8, EY), 0)

    def block(j):
        return slice(j * EY, (j + 1) * EY)

    def pack(f, _):
        rows = pl.ds(pl.multiple_of(f * Q, Q), Q)
        low = jnp.zeros((Q, EY), F32)
        high = jnp.zeros((Q, EY), F32)
        for j in range(EX):
            values = u_ref[rows, block(j)]
            low = jnp.where(lane64 == j, pltpu.roll(values, j, 1) if j else values, low)
            high = jnp.where(lane64 == j, pltpu.roll(values, j + 1, 1), high)
        packed[0, rows, :] = low
        packed[1, rows, :] = high
        return 0

    lax.fori_loop(0, F, pack, 0)
    pl.semaphore_wait(barrier, len(partners))
    for p in range(3):
        for s in range(4):
            side_copy(p, s).start()
    fold(inverse_ref, [own_ref[s] for s in range(4)] + [next_ref[s] for s in range(4)], g_ref)
    fold(inverse_ref, [project_ref[k] for k in range(4)], p_ref)

    def interior(f, _):
        rows = pl.ds(pl.multiple_of(f * Q, Q), Q)
        u = u_ref[rows, :]
        made = product(g_ref[...], u)
        for j in range(EX):
            total = u[:, block(j)]
            for s in range(4):
                outward = jnp.maximum(v_ref[s, j : j + 1, :], 0.0)
                total = total - outward * made[s * Q : (s + 1) * Q, block(j)]
            inward = [jnp.minimum(v_ref[s, j : j + 1, :], 0.0) for s in range(4)]
            if j > 0:
                total = total - inward[0] * made[4 * Q : 5 * Q, block(j - 1)]
            if j < EX - 1:
                total = total - inward[1] * made[5 * Q : 6 * Q, block(j + 1)]
            before = pltpu.roll(made[6 * Q : 7 * Q, block(j)], 1, 1)
            after = pltpu.roll(made[7 * Q : 8 * Q, block(j)], EY - 1, 1)
            total = total - jnp.where(lane64 == 0, 0.0, inward[2] * before)
            total = total - jnp.where(lane64 == EY - 1, 0.0, inward[3] * after)
            lim_ref[rows, block(j)] = total
        return 0

    lax.fori_loop(0, F, interior, 0)

    def edges(p):
        first, count, _ = PARTS[p]
        for s in range(4):
            side_copy(p, s).wait_recv()

        def field(f, found):
            found = list(found)
            rows = pl.ds(pl.multiple_of((first + f) * Q, Q), Q)
            made = [
                product(g_ref[(4 + s) * Q : (5 + s) * Q, :], sides[s, rows, :]) for s in range(4)
            ]
            for j in range(EX):
                inward = [jnp.minimum(v_ref[s, j : j + 1, :], 0.0) * gate[s] for s in range(4)]
                total = lim_ref[rows, block(j)]
                if j == 0:
                    total = total - inward[0] * made[0]
                if j == EX - 1:
                    total = total - inward[1] * made[1]
                before = made[2] if j == 0 else pltpu.roll(made[2], EY - j, 1)
                after = pltpu.roll(made[3], EY - 1 - j, 1)
                total = total - jnp.where(lane64 == 0, inward[2] * before, 0.0)
                total = total - jnp.where(lane64 == EY - 1, inward[3] * after, 0.0)
                lim_ref[rows, block(j)] = total
                mean = jnp.sum(total, axis=0, keepdims=True) * (1.0 / Q)
                found[j] = jnp.where(row8 == f, mean, found[j])
            return tuple(found)

        found = lax.fori_loop(
            0, count, field, tuple(jnp.zeros((8, EY), F32) for _ in range(EX))
        )
        low = jnp.zeros((8, EY), F32)
        high = jnp.zeros((8, EY), F32)
        for j in range(EX):
            means[p, :, block(j)] = found[j]
            low = jnp.where(lane8 == j, pltpu.roll(found[j], j, 1) if j else found[j], low)
            high = jnp.where(lane8 == j, pltpu.roll(found[j], j + 1, 1), high)
        mean_packed[p, 0] = low
        mean_packed[p, 1] = high
        for s in range(4):
            mean_copy(p, s).start()

    def limit(p):
        first, count, _ = PARTS[p]
        for s in range(4):
            mean_copy(p, s).wait_recv()
        for j in range(EX):
            center = means[p, :, block(j)]
            if j > 0:
                left = means[p, :, block(j - 1)]
            else:
                left = jnp.where(gate[0] > 0, mean_sides[p, 0], center)
            if j < EX - 1:
                right = means[p, :, block(j + 1)]
            else:
                right = jnp.where(gate[1] > 0, mean_sides[p, 1], center)
            before = mean_sides[p, 2] if j == 0 else pltpu.roll(mean_sides[p, 2], EY - j, 1)
            before = jnp.where(gate[2] > 0, before, center)
            before = jnp.where(lane8 == 0, before, pltpu.roll(center, 1, 1))
            after = pltpu.roll(mean_sides[p, 3], EY - 1 - j, 1)
            after = jnp.where(gate[3] > 0, after, center)
            after = jnp.where(lane8 == EY - 1, after, pltpu.roll(center, EY - 1, 1))
            lower, upper = center, center
            for other in (left, right, before, after):
                lower = jnp.minimum(lower, other)
                upper = jnp.maximum(upper, other)
            lower, upper = lower - MARGIN, upper + MARGIN
            for f in range(count):
                rows = slice((first + f) * Q, (first + f + 1) * Q)
                values = jnp.maximum(lim_ref[rows, block(j)], lower[f : f + 1])
                lim_ref[rows, block(j)] = jnp.minimum(values, upper[f : f + 1])
        for d in (2, 1, 3):
            states_copy(p, d).start()

    edges(0)
    edges(1)
    limit(0)
    edges(2)
    limit(1)
    limit(2)

    table = rank_table(rows_ref)
    for p in range(3):
        axes = PARTS[p][2]
        part_table(table, axes, tables[p])
        at[p][0] = tables[p][here[axes[0]]]
        for d in (2, 1, 3):
            table_copy(p, d).start()

    element = lax.broadcasted_iota(jnp.int32, (E, 256), 0).astype(F32)
    quarter = lax.rem(lax.broadcasted_iota(jnp.int32, (1, 256), 1) // CAP, 4)

    def route(p):
        first, count, axes = PARTS[p]
        rows = count * Q
        me_b = here[axes[1]]
        for d in (0, 1, 3, 2):
            if d:
                states_copy(p, d).wait_recv()
                table_copy(p, d).wait_recv()
            j = (4 - d) % 4
            values = lim_ref[first * Q : first * Q + rows, :] if d == 0 else ar[p][3 - d]
            high, low = halves(values)
            split[j, 0:rows, :] = high
            split[j, rows : 2 * rows, :] = low

        def towards(step, _):
            d = 3 - step
            group = lax.rem(me_b + d, 4) * 2

            def info_of(j, what):
                tile = at[p][j, what]
                lanes = []
                for core in range(2):
                    row = jnp.where(row8 == group + core, tile, 0.0)
                    row = jnp.sum(row, axis=0, keepdims=True)
                    lanes.append(pltpu.roll(row, CAP * j, 1) if j else row)
                return jnp.concatenate(lanes, axis=1)

            infos = []
            for j in range(4):
                infos.append([info_of(j, what) for what in (1, 2, 3)])
                hot = jnp.where(element == info_of(j, 0), 1.0, 0.0).astype(BF16)
                made = jnp.dot(split[j, 0 : 2 * rows, :], hot, preferred_element_type=F32)
                picked[j, 0:rows, :] = made[0:rows] + made[rows:]
            for o in range(4):
                which, slot, weight = infos[3]
                for j in range(3):
                    mine = quarter == (o + j) % 4
                    which = jnp.where(mine, infos[j][0], which)
                    slot = jnp.where(mine, infos[j][1], slot)
                    weight = jnp.where(mine, infos[j][2], weight)
                for f in range(count):
                    part = slice(f * Q, (f + 1) * Q)
                    values = picked[3, part, :]
                    for j in range(3):
                        values = jnp.where(quarter == (o + j) % 4, picked[j, part, :], values)
                    made = product(p_ref[...], values)
                    chosen = made[3 * Q :]
                    for k in range(3):
                        chosen = jnp.where(which == float(k), made[k * Q : (k + 1) * Q], chosen)
                    chosen = chosen * weight
                    bs[p][d, 0, o, part, :] = chosen[:, 0:128]
                    bs[p][d, 1, o, part, :] = chosen[:, 128:256]
                slot = jnp.broadcast_to(slot, (8, 256))
                bs[p][d, 0, o, rows : rows + 8, :] = slot[:, 0:128]
                bs[p][d, 1, o, rows : rows + 8, :] = slot[:, 128:256]
            block_copy(p, d, 1).start()

            @pl.when(d > 0)
            def _():
                block_copy(p, d, 0).start()

            return 0

        lax.fori_loop(0, 4, towards, 0)
        own_copy(p).start()

    def gather(p):
        _, count, axes = PARTS[p]
        rows = count * Q
        me_c = here[axes[2]]
        for number, d in enumerate((0, 1, 3, 2)):
            if d == 0:
                own_copy(p).wait()
                block_copy(p, 0, 1).wait_recv()
            else:
                block_copy(p, d, 0).wait_recv()
                block_copy(p, d, 1).wait_recv()
            slot_of = (4 - d) % 4

            def owner(step, _, number=number, slot_of=slot_of):
                distance = lax.rem(step + 2, 4)
                o = lax.rem(me_c + distance, 4)
                high, low = halves(br[p][slot_of, o, 0:rows, :])
                pair[0:rows, :] = high
                pair[rows : 2 * rows, :] = low
                hot = jnp.where(element == br[p][slot_of, o, rows : rows + 1, :], 1.0, 0.0)
                made = lax.dot_general(
                    pair[0 : 2 * rows, :],
                    hot.astype(BF16),
                    (((1,), (1,)), ((), ())),
                    preferred_element_type=F32,
                )
                total = made[0:rows] + made[rows:]
                if number > 0:
                    total = total + cs[p][o]
                cs[p][o] = total
                if number == 3:

                    @pl.when(distance > 0)
                    def _():
                        sum_copy(p, distance).start()

                return 0

            lax.fori_loop(0, 4, owner, 0)

    def finish(p):
        first, count, axes = PARTS[p]
        total = cs[p][here[axes[2]]]
        for d in (1, 3, 2):
            sum_copy(p, d).wait_recv()
            total = total + cr[p][d - 1]
        out_ref[first * Q : (first + count) * Q, :] = total

    for p in range(3):
        route(p)
    for p in (2, 0, 1):
        gather(p)
    for p in (2, 0, 1):
        finish(p)
    for p in range(3):
        for s in range(4):
            side_copy(p, s).wait_send()
            mean_copy(p, s).wait_send()
        for d in (1, 2, 3):
            states_copy(p, d).wait_send()
            table_copy(p, d).wait_send()
            block_copy(p, d, 0).wait_send()
            block_copy(p, d, 1).wait_send()
            sum_copy(p, d).wait_send()
        block_copy(p, 0, 1).wait_send()


def body(
    states,
    swept_volume,
    flux_own,
    flux_next,
    mass_inverse,
    projection,
    new_owner,
    new_slot,
    intersection_weight,
):
    owner = new_owner.reshape(E, K).T.reshape(E * K)
    slot = new_slot.reshape(E, K).T.reshape(E * K)
    weight = intersection_weight.reshape(E, K).T.reshape(E * K)
    which = jnp.arange(E * K, dtype=jnp.int32)
    element = which % E + 1
    listing = jnp.stack(
        [
            owner.astype(F32),
            (element // 128).astype(F32),
            (element % 128).astype(F32),
            (which // E).astype(F32),
            (slot // 128).astype(F32),
            (slot % 128).astype(F32),
            weight,
            jnp.zeros((E * K,), F32),
        ]
    )
    rows = [count * Q for _, count, _ in PARTS]
    dma = pltpu.SemaphoreType.DMA
    made = pl.pallas_call(
        kernel,
        out_shape=jax.ShapeDtypeStruct((COLS, E), F32),
        in_specs=[VMEM] * 7,
        out_specs=VMEM,
        scratch_shapes=[
            pltpu.VMEM((8 * Q, 3 * Q), BF16),
            pltpu.VMEM((4 * Q, 3 * Q), BF16),
            pltpu.VMEM((COLS, E), F32),
            pltpu.VMEM((4, COLS, EY), F32),
            pltpu.VMEM((2, COLS, EY), F32),
            pltpu.VMEM((3, 8, E), F32),
            pltpu.VMEM((3, 4, 8, EY), F32),
            pltpu.VMEM((3, 2, 8, EY), F32),
        ]
        + [pltpu.VMEM((4, 4, 8, 128), F32) for r in rows]
        + [pltpu.VMEM((3, r, E), F32) for r in rows]
        + [pltpu.VMEM((4, 4, 8, 128), F32) for r in rows]
        + [pltpu.VMEM((4, 2, 4, r + 8, 128), F32) for r in rows]
        + [pltpu.VMEM((4, 4, r + 8, 256), F32) for r in rows]
        + [pltpu.VMEM((4, r, E), F32) for r in rows]
        + [pltpu.VMEM((3, r, E), F32) for r in rows]
        + [
            pltpu.VMEM((4, 2 * max(rows), E), BF16),
            pltpu.VMEM((4, max(rows), 256), F32),
            pltpu.VMEM((2 * max(rows), 256), BF16),
            dma((3, 4)),
            dma((3, 4)),
            dma((3, 4)),
            dma((3, 4)),
            dma((3, 3)),
            dma((3, 3)),
            dma((3, 3)),
            dma((3, 3)),
            dma((3, 4, 2)),
            dma((3, 4, 2)),
            dma((3, 3)),
            dma((3, 3)),
            dma((3,)),
        ],
        compiler_params=pltpu.CompilerParams(
            collective_id=0, has_side_effects=True, vmem_limit_bytes=56 * 2**20
        ),
    )(
        states.reshape(COLS, E),
        swept_volume,
        mass_inverse,
        flux_own,
        flux_next,
        projection,
        listing,
    )
    return made.reshape(F, Q, E)


def solution(mesh):
    placed = (
        P(None, None, "gx", "gy"),
        P(None, "gx", "gy"),
        P(),
        P(),
        P(),
        P(),
        P("gx", "gy", None, None),
        P("gx", "gy", None, None),
        P("gx", "gy", None, None),
    )
    return jax.shard_map(
        body, mesh=mesh, in_specs=placed, out_specs=P(None, None, ("gx", "gy")), check_vma=False
    )
```

time: 277 us -> 121 us (0.44); the launches traced: 272 us -> 120 us
  Pallas kernels: 0 us -> 113 us
  waiting for transfers between devices: 104 us -> 0 us
  local copies, waits for them, and re-layouts: 61.7 us -> 6.64 us
  starting transfers between devices: 46.7 us -> 0 us
  matrix products: 29.6 us -> 0 us
  other arithmetic: 29.2 us -> 0.81 us
    pallas_call x0 -> x1, Pallas kernels: none -> 113 us  [body(): pl.pallas_call(kernel, out_shape=jax.ShapeDtypeStruct((COLS, E), F32), in...]
    all_to_all x2 -> x0, waiting for transfers between devices: 97.9 us -> none  [the longest x1 97.9 us: body(): lax.all_to_all(outgoing, ('gx', 'gy'), split_axis=0, concat_axis=0, tiled...]
    all_to_all x2 -> x0, starting transfers between devices: 30.4 us -> none  [the longest x1 15.5 us: body(): lax.all_to_all(places, ('gx', 'gy'), split_axis=0, concat_axis=0, tiled=T...]
    dot_general x11 -> x0, matrix products: 29.6 us -> none  [the longest x9 22.6 us: nodal_product(): return jnp.einsum('pq,fqxy->fpxy', matrix, values, precision=PRECISE)]
    scatter x6 -> x0, local copies, waits for them, and re-layouts: 27.1 us -> none  [the longest x1 13.4 us: body(): jnp.zeros((devices * capacity, width_all), jnp.float32).at[position]]
    scatter-add x1 -> x0, other arithmetic: 26.1 us -> none  [body(): jnp.zeros((old_count, width_all), jnp.float32).at[arrived.astype(jnp.int32)]]
    ppermute x8 -> x0, starting transfers between devices: 16.3 us -> none  [the longest x4 10.7 us: with_halo(): lax.ppermute(tail, axis, [(i, (i + 1) % count) for i in range(ends)])]
    mul x3 -> x0, local copies, waits for them, and re-layouts: 10.1 us -> none  [the longest x1 9.13 us: body(): jnp.einsum('kpq,fqe->ekfp', projection, flat_state, precision=PRECISE)]
  transfers between devices with their start and end apart: 10 -> 0, of which waited for: 3 -> 0; matrix products, arithmetic and copies ran while one was open for 29% -> 0% of each run, Pallas kernels for 0% -> 0%
where the time goes in v2:
time: 121 us; the launch traced here: 120 us
  Pallas kernels  113 us (93%)
  local copies, waits for them, and re-layouts  6.64 us (5%)
    pallas_call x1, Pallas kernels, body(): pl.pallas_call(kernel, out_shape=jax.ShapeDtypeStruct((COLS, E), F32), in...  113 us
    unnamed x9, local copies, waits for them, and re-layouts  5.92 us

profile of v2, /device:TPU:0, one launch (start us, length us, event | category | flops | bytes accessed | tf_op | source)
XLA Modules:
  0.0 120.3 jit_solution(16833749433881911016)
XLA Ops:
  0.0 0.7 convert_bitcast_fusion
  0.7 0.0 copy-start
  0.7 0.7 copy-done
  1.4 0.0 copy-start.1
  1.4 0.7 copy-done.1
  2.3 0.7 stack.2.rows_ref
  3.0 2.3 %copy.15 = f32[64,8,4,128]{3,1,2,0:T(8,128)} copy(f32[64,8,4,128]{3,2,1,0:T(4,128)} %bitcast.27) | data formatting | bytes 2097152
  5.2 112.8 %shard_map.91 = f32[512,512]{1,0:T(8,128)} custom-call(f32[512,512]{1,0:T(8,128)} %bitcast.26, f32[4,4,128]{2,1,0:T(4,128)} %v_ref.1, f32[64,64]{1,0:T(8,128)} %inverse_ref.1, f32[4,64,64]{2,1,0:T(8,128)} %own_ref.1, f32[4,64,64]{2,1,0:T(8,128)} %next_ref.1, f32[4,64,64]{2,1,0:T(8,128)} %project_ref.1, f32[8,2048]{1,0:T(8,128)} %stack.2.rows_ref), custom_call_target="tpu_custom_call" | custom-call | tf_op jit(solution)/shard_map/pallas_call | solution.py:519
  118.1 2.3 %copy.17 = f32[8,64,512]{2,1,0:T(8,128)} copy(f32[8,64,512]{2,1,0:T(8,128)} %bitcast.25) | data formatting | bytes 2097152
  (7 shorter events, 0.1 us)
Async XLA Ops:
  0.7 0.7 copy-start
  1.4 0.7 copy-start.1

commit v3 on v2

--- a/solution.py
+++ b/solution.py
@@ -99,15 +99,17 @@
 
 
 def kernel(
-    u_ref, v_ref, inverse_ref, own_ref, next_ref, project_ref, rows_ref, out_ref,
-    g_ref, p_ref, lim_ref, sides, packed, means, mean_sides, mean_packed,
+    states_ref, v_ref, inverse_ref, own_ref, next_ref, project_ref, rows_ref, out0, out1, out2,
+    u_ref, g_ref, p_ref, lim_ref, sides, packed, means, mean_sides, mean_packed,
     tb0, tb1, tb2, ar0, ar1, ar2, at0, at1, at2, bs0, bs1, bs2, br0, br1, br2,
-    cs0, cs1, cs2, cr0, cr1, cr2, split, picked, pair,
-    h_send, h_recv, m_send, m_recv,
-    a_send, a_recv, t_send, t_recv, b_send, b_recv, c_send, c_recv, own_sem,
+    cs0, cs1, cs2, cr0, cr1, cr2, ct0, ct1, ct2, split, picked, pair,
+    u_sem, h_send, h_recv, m_send, m_recv,
+    a_send, a_recv, f_send, f_recv, t_send, t_recv, b_send, b_recv, c_send, c_recv, d_send, d_recv,
+    own_sem,
 ):
     tables, ar, at = (tb0, tb1, tb2), (ar0, ar1, ar2), (at0, at1, at2)
     bs, br, cs, cr = (bs0, bs1, bs2), (br0, br1, br2), (cs0, cs1, cs2), (cr0, cr1, cr2)
+    ct, out = (ct0, ct1, ct2), (out0, out1, out2)
     gx, gy = lax.axis_index("gx"), lax.axis_index("gy")
     n_x, n_y = lax.axis_size("gx"), lax.axis_size("gy")
     here = {"x": gy // 2, "y": lax.rem(gx, 4), "z": gx // 4, "c": lax.rem(gy, 2)}
@@ -128,6 +130,14 @@
 
     partners = [away(axis, d, core) for axis in "xyz" for d in (1, 2, 3) for core in (0, 1)]
     partners += [away("x", 0, 1), *near]
+    loads = [
+        pltpu.make_async_copy(
+            states_ref.at[:, j, :], u_ref.at[:, pl.ds(j * EY, EY)], u_sem.at[j]
+        )
+        for j in range(EX)
+    ]
+    for load in loads:
+        load.start()
     barrier = pltpu.get_barrier_semaphore()
     for device in partners:
         pl.semaphore_signal(barrier, inc=1, device_id=device, device_id_type=MESH)
@@ -169,12 +179,28 @@
             source, mean_sides.at[p, s ^ 1], m_send.at[p, s], m_recv.at[p, s ^ 1], near[s]
         )
 
-    def states_copy(p, d):
-        return remote(
-            lim_ref.at[rows_of(p)],
-            ar[p].at[3 - d],
-            a_send.at[p, d - 1],
-            a_recv.at[p, d - 1],
+    def half_of(p, h):
+        size = PARTS[p][1] * Q // 2
+        return pl.ds(h * size, size)
+
+    def states_copy(p, d, h):
+        first, count, axes = PARTS[p]
+        size = count * Q // 2
+        return remote(
+            lim_ref.at[pl.ds(first * Q + h * size, size)],
+            ar[p].at[3 - d, half_of(p, h)],
+            a_send.at[p, d // 2, h],
+            a_recv.at[p, d // 2, h],
+            away(axes[0], d),
+        )
+
+    def relay_copy(p, d):
+        half = half_of(p, d // 2)
+        return remote(
+            ar[p].at[3 - d, half],
+            ar[p].at[1, half],
+            f_send.at[p, d // 2],
+            f_recv.at[p, d // 2],
             away(PARTS[p][2][0], d),
         )
 
@@ -191,7 +217,7 @@
     def block_copy(p, d, core):
         return remote(
             bs[p].at[d, lax.rem(here["c"] + core, 2)],
-            br[p].at[lax.rem(4 - d, 4), :, :, pl.ds(core * 128, 128)],
+            br[p].at[lax.rem(4 - d, 4), :, pl.ds(core * 128, 128)],
             b_send.at[p, d, core],
             b_recv.at[p, d, core],
             away(PARTS[p][2][1], d, core),
@@ -199,22 +225,35 @@
 
     def own_copy(p):
         return pltpu.make_async_copy(
-            bs[p].at[0, here["c"]], br[p].at[0, :, :, pl.ds(0, 128)], own_sem.at[p]
-        )
-
-    def sum_copy(p, d):
-        axis = PARTS[p][2][2]
-        return remote(
-            cs[p].at[lax.rem(here[axis] + d, 4)],
-            cr[p].at[d - 1],
-            c_send.at[p, d - 1],
-            c_recv.at[p, d - 1],
-            away(axis, d),
+            bs[p].at[0, here["c"]], br[p].at[0, :, pl.ds(0, 128)], own_sem.at[p]
+        )
+
+    def owner_at(p, d):
+        return lax.rem(here[PARTS[p][2][2]] + d, 4)
+
+    def far_sum(p, d):
+        return remote(
+            cs[p].at[owner_at(p, 2), half_of(p, d // 2)],
+            ct[p].at[d // 2],
+            d_send.at[p, d // 2],
+            d_recv.at[p, d // 2],
+            away(PARTS[p][2][2], d),
+        )
+
+    def near_sum(p, d, h):
+        half = half_of(p, h)
+        return remote(
+            cs[p].at[owner_at(p, d), half],
+            cr[p].at[d // 2, half],
+            c_send.at[p, d // 2, h],
+            c_recv.at[p, d // 2, h],
+            away(PARTS[p][2][2], d),
         )
 
     lane64 = lax.broadcasted_iota(jnp.int32, (Q, EY), 1)
     lane8 = lax.broadcasted_iota(jnp.int32, (8, EY), 1)
     row8 = lax.broadcasted_iota(jnp.int32, (8, EY), 0)
+    row256 = lax.broadcasted_iota(jnp.int32, (8, 256), 0)
 
     def block(j):
         return slice(j * EY, (j + 1) * EY)
@@ -231,6 +270,8 @@
         packed[1, rows, :] = high
         return 0
 
+    for load in loads:
+        load.wait()
     lax.fori_loop(0, F, pack, 0)
     pl.semaphore_wait(barrier, len(partners))
     for p in range(3):
@@ -332,15 +373,14 @@
                 rows = slice((first + f) * Q, (first + f + 1) * Q)
                 values = jnp.maximum(lim_ref[rows, block(j)], lower[f : f + 1])
                 lim_ref[rows, block(j)] = jnp.minimum(values, upper[f : f + 1])
-        for d in (2, 1, 3):
-            states_copy(p, d).start()
-
-    edges(0)
-    edges(1)
-    limit(0)
-    edges(2)
-    limit(1)
-    limit(2)
+        for h in (0, 1):
+            states_copy(p, 1, h).start()
+            states_copy(p, 3, 1 - h).start()
+
+    for p in range(3):
+        edges(p)
+    for p in range(3):
+        limit(p)
 
     table = rank_table(rows_ref)
     for p in range(3):
@@ -349,6 +389,10 @@
         at[p][0] = tables[p][here[axes[0]]]
         for d in (2, 1, 3):
             table_copy(p, d).start()
+    for p in range(3):
+        for d in (1, 3):
+            states_copy(p, d, d // 2).wait_recv()
+            relay_copy(p, d).start()
 
     element = lax.broadcasted_iota(jnp.int32, (E, 256), 0).astype(F32)
     quarter = lax.rem(lax.broadcasted_iota(jnp.int32, (1, 256), 1) // CAP, 4)
@@ -359,8 +403,12 @@
         me_b = here[axes[1]]
         for d in (0, 1, 3, 2):
             if d:
-                states_copy(p, d).wait_recv()
                 table_copy(p, d).wait_recv()
+            if d == 2:
+                relay_copy(p, 1).wait_recv()
+                relay_copy(p, 3).wait_recv()
+            elif d:
+                states_copy(p, d, 1 - d // 2).wait_recv()
             j = (4 - d) % 4
             values = lim_ref[first * Q : first * Q + rows, :] if d == 0 else ar[p][3 - d]
             high, low = halves(values)
@@ -386,6 +434,7 @@
                 hot = jnp.where(element == info_of(j, 0), 1.0, 0.0).astype(BF16)
                 made = jnp.dot(split[j, 0 : 2 * rows, :], hot, preferred_element_type=F32)
                 picked[j, 0:rows, :] = made[0:rows] + made[rows:]
+            slots = jnp.zeros((8, 256), F32)
             for o in range(4):
                 which, slot, weight = infos[3]
                 for j in range(3):
@@ -403,11 +452,12 @@
                     for k in range(3):
                         chosen = jnp.where(which == float(k), made[k * Q : (k + 1) * Q], chosen)
                     chosen = chosen * weight
-                    bs[p][d, 0, o, part, :] = chosen[:, 0:128]
-                    bs[p][d, 1, o, part, :] = chosen[:, 128:256]
-                slot = jnp.broadcast_to(slot, (8, 256))
-                bs[p][d, 0, o, rows : rows + 8, :] = slot[:, 0:128]
-                bs[p][d, 1, o, rows : rows + 8, :] = slot[:, 128:256]
+                    place = slice(o * rows + f * Q, o * rows + (f + 1) * Q)
+                    bs[p][d, 0, place, :] = chosen[:, 0:128]
+                    bs[p][d, 1, place, :] = chosen[:, 128:256]
+                slots = jnp.where(row256 == o, slot, slots)
+            bs[p][d, 0, 4 * rows : 4 * rows + 8, :] = slots[:, 0:128]
+            bs[p][d, 1, 4 * rows : 4 * rows + 8, :] = slots[:, 128:256]
             block_copy(p, d, 1).start()
 
             @pl.when(d > 0)
@@ -432,13 +482,15 @@
                 block_copy(p, d, 1).wait_recv()
             slot_of = (4 - d) % 4
 
-            def owner(step, _, number=number, slot_of=slot_of):
-                distance = lax.rem(step + 2, 4)
+            def owner(distance, number=number, slot_of=slot_of):
                 o = lax.rem(me_c + distance, 4)
-                high, low = halves(br[p][slot_of, o, 0:rows, :])
+                place = pl.ds(pl.multiple_of(o * rows, rows), rows)
+                high, low = halves(br[p][slot_of, place, :])
                 pair[0:rows, :] = high
                 pair[rows : 2 * rows, :] = low
-                hot = jnp.where(element == br[p][slot_of, o, rows : rows + 1, :], 1.0, 0.0)
+                slot = br[p][slot_of, 4 * rows : 4 * rows + 8, :]
+                slot = jnp.sum(jnp.where(row256 == o, slot, 0.0), axis=0, keepdims=True)
+                hot = jnp.where(element == slot, 1.0, 0.0)
                 made = lax.dot_general(
                     pair[0 : 2 * rows, :],
                     hot.astype(BF16),
@@ -449,40 +501,65 @@
                 if number > 0:
                     total = total + cs[p][o]
                 cs[p][o] = total
-                if number == 3:
-
-                    @pl.when(distance > 0)
-                    def _():
-                        sum_copy(p, distance).start()
-
-                return 0
-
-            lax.fori_loop(0, 4, owner, 0)
+
+            if number < 3:
+
+                def step(distance, _, owner=owner):
+                    owner(distance)
+                    return 0
+
+                lax.fori_loop(0, 4, step, 0)
+            else:
+                owner(2)
+                far_sum(p, 1).start()
+                far_sum(p, 3).start()
+                owner(1)
+                near_sum(p, 1, 1).start()
+                owner(3)
+                near_sum(p, 3, 0).start()
+                owner(0)
+
+    def combine(p):
+        half = PARTS[p][1] * Q // 2
+        for d in (1, 3):
+            far_sum(p, d).wait_recv()
+            o = owner_at(p, d)
+            place = slice((d // 2) * half, (d // 2 + 1) * half)
+            cs[p][o, place, :] = cs[p][o, place, :] + ct[p][d // 2]
+            near_sum(p, d, d // 2).start()
 
     def finish(p):
-        first, count, axes = PARTS[p]
-        total = cs[p][here[axes[2]]]
-        for d in (1, 3, 2):
-            sum_copy(p, d).wait_recv()
-            total = total + cr[p][d - 1]
-        out_ref[first * Q : (first + count) * Q, :] = total
+        total = cs[p][here[PARTS[p][2][2]]]
+        for d in (1, 3):
+            for h in (0, 1):
+                near_sum(p, d, h).wait_recv()
+            total = total + cr[p][d // 2]
+        out[p][...] = total
 
     for p in range(3):
         route(p)
-    for p in (2, 0, 1):
-        gather(p)
+    gather(2)
+    combine(2)
+    gather(0)
+    gather(1)
+    for p in (0, 1):
+        combine(p)
     for p in (2, 0, 1):
         finish(p)
     for p in range(3):
         for s in range(4):
             side_copy(p, s).wait_send()
             mean_copy(p, s).wait_send()
+        for d in (1, 3):
+            for h in (0, 1):
+                states_copy(p, d, h).wait_send()
+                near_sum(p, d, h).wait_send()
+            relay_copy(p, d).wait_send()
+            far_sum(p, d).wait_send()
         for d in (1, 2, 3):
-            states_copy(p, d).wait_send()
             table_copy(p, d).wait_send()
             block_copy(p, d, 0).wait_send()
             block_copy(p, d, 1).wait_send()
-            sum_copy(p, d).wait_send()
         block_copy(p, 0, 1).wait_send()
 
 
@@ -518,10 +595,11 @@
     dma = pltpu.SemaphoreType.DMA
     made = pl.pallas_call(
         kernel,
-        out_shape=jax.ShapeDtypeStruct((COLS, E), F32),
-        in_specs=[VMEM] * 7,
-        out_specs=VMEM,
+        out_shape=[jax.ShapeDtypeStruct((r, E), F32) for r in rows],
+        in_specs=[pl.BlockSpec(memory_space=pl.ANY)] + [VMEM] * 6,
+        out_specs=[VMEM] * 3,
         scratch_shapes=[
+            pltpu.VMEM((COLS, E), F32),
             pltpu.VMEM((8 * Q, 3 * Q), BF16),
             pltpu.VMEM((4 * Q, 3 * Q), BF16),
             pltpu.VMEM((COLS, E), F32),
@@ -534,33 +612,30 @@
         + [pltpu.VMEM((4, 4, 8, 128), F32) for r in rows]
         + [pltpu.VMEM((3, r, E), F32) for r in rows]
         + [pltpu.VMEM((4, 4, 8, 128), F32) for r in rows]
-        + [pltpu.VMEM((4, 2, 4, r + 8, 128), F32) for r in rows]
-        + [pltpu.VMEM((4, 4, r + 8, 256), F32) for r in rows]
+        + [pltpu.VMEM((4, 2, 4 * r + 8, 128), F32) for r in rows]
+        + [pltpu.VMEM((4, 4 * r + 8, 256), F32) for r in rows]
         + [pltpu.VMEM((4, r, E), F32) for r in rows]
-        + [pltpu.VMEM((3, r, E), F32) for r in rows]
+        + [pltpu.VMEM((2, r, E), F32) for r in rows]
+        + [pltpu.VMEM((2, r // 2, E), F32) for r in rows]
         + [
             pltpu.VMEM((4, 2 * max(rows), E), BF16),
             pltpu.VMEM((4, max(rows), 256), F32),
             pltpu.VMEM((2 * max(rows), 256), BF16),
-            dma((3, 4)),
-            dma((3, 4)),
-            dma((3, 4)),
-            dma((3, 4)),
-            dma((3, 3)),
-            dma((3, 3)),
-            dma((3, 3)),
-            dma((3, 3)),
-            dma((3, 4, 2)),
-            dma((3, 4, 2)),
-            dma((3, 3)),
-            dma((3, 3)),
+            dma((4,)),
+            *[dma((3, 4))] * 4,
+            *[dma((3, 2, 2))] * 2,
+            *[dma((3, 2))] * 2,
+            *[dma((3, 3))] * 2,
+            *[dma((3, 4, 2))] * 2,
+            *[dma((3, 2, 2))] * 2,
+            *[dma((3, 2))] * 2,
             dma((3,)),
         ],
         compiler_params=pltpu.CompilerParams(
             collective_id=0, has_side_effects=True, vmem_limit_bytes=56 * 2**20
         ),
     )(
-        states.reshape(COLS, E),
+        states.reshape(COLS, EX, EY),
         swept_volume,
         mass_inverse,
         flux_own,
@@ -568,7 +643,7 @@
         projection,
         listing,
     )
-    return made.reshape(F, Q, E)
+    return jnp.concatenate(made, axis=0).reshape(F, Q, E)
 
 
 def solution(mesh):

time: 121 us -> 109 us (0.901)
  the two profiles are of different devices: /device:TPU:0 before, /device:TPU:106 now
where the time goes in v3:
time: 109 us
  Pallas kernels  104 us (95%)
  other arithmetic  3.05 us (3%)
  local copies, waits for them, and re-layouts  2.13 us (2%)
    pallas_call x1, Pallas kernels, body(): pl.pallas_call(kernel, out_shape=[jax.ShapeDtypeStruct((r, E), F32) for r...  104 us
    concatenate x1, other arithmetic, body(): return jnp.concatenate(made, axis=0).reshape(F, Q, E)  2.23 us

profile of v3, /device:TPU:106, one launch (start us, length us, event | category | flops | bytes accessed | tf_op | source)
XLA Modules:
  0.0 109.1 jit_solution(742142045411508636)
XLA Ops:
  0.0 0.7 convert_bitcast_fusion
  0.7 0.0 copy-start
  0.7 0.7 copy-done
  1.4 0.0 copy-start.1
  1.4 0.7 copy-done.1
  2.3 0.7 stack.2.rows_ref
  3.0 103.9 %shard_map.91 = (f32[192,512]{1,0:T(8,128)}, f32[192,512]{1,0:T(8,128)}, f32[128,512]{1,0:T(8,128)}) custom-call(f32[512,4,128]{2,1,0:T(4,128)} %bitcast.21, f32[4,4,128]{2,1,0:T(4,128)} %v_ref.1, f32[64,64]{1,0:T(8,128)} %inverse_ref.1, f32[4,64,64]{2,1,0:T(8,128)} %own_ref.1, f32[4,64,64]{2,1,0:T(8,128)} %next_ref.1, f32[4,64,64]{2,1,0:T(8,128)} %project_ref.1, ...), custom_call_target="tpu_custom_call" | custom-call | tf_op jit(solution)/shard_map/pallas_call | solution.py:596
  106.9 2.2 %pad_maximum_fusion = f32[512,512]{1,0:T(8,128)} fusion(f32[128,512]{1,0:T(8,128)} %get-tuple-element.10, f32[192,512]{1,0:T(8,128)} %get-tuple-element.9, f32[192,512]{1,0:T(8,128)} %get-tuple-element.8), kind=kLoop, calls=%fused_computation | loop fusion | flops 524288 | bytes 2097152 | tf_op jit(solution)/shard_map/concatenate | solution.py:646
  (7 shorter events, 0.1 us)
Async XLA Ops:
  0.7 0.7 copy-start
  1.4 0.7 copy-start.1

commit v4 on v3

--- a/solution.py
+++ b/solution.py
@@ -13,6 +13,7 @@
 MARGIN = 0.75
 MESH = pl.DeviceIdType.MESH
 VMEM = pl.BlockSpec(memory_space=pltpu.VMEM)
+HBM = pl.BlockSpec(memory_space=pltpu.HBM)
 F32, BF16 = jnp.float32, jnp.bfloat16
 PARTS = ((0, 3, "xyz"), (3, 3, "yzx"), (6, 2, "zxy"))
 
@@ -38,8 +39,8 @@
         target_ref[term * Q : (term + 1) * Q, :] = jnp.concatenate([high, high, low], axis=1)
 
 
-def rank_table(rows_ref):
-    devices = lax.broadcasted_iota(jnp.int32, (128, 256), 0).astype(F32)
+def rank_table(owner_ref, slot_ref, weight_ref):
+    devices = lax.broadcasted_iota(jnp.int32, (128, 256), 0)
     ranks = lax.broadcasted_iota(jnp.int32, (CAP, 256), 0).astype(F32)
     earlier = lax.broadcasted_iota(jnp.int32, (256, 256), 0) < lax.broadcasted_iota(
         jnp.int32, (256, 256), 1
@@ -47,25 +48,36 @@
     earlier = jnp.where(earlier, 1.0, 0.0).astype(BF16)
     carry = jnp.zeros((128, 1), F32)
     table = jnp.zeros((128, 8 * CAP), F32)
-    for chunk in range(E * K // 256):
-        lanes = slice(chunk * 256, (chunk + 1) * 256)
-        named = jnp.where(devices == rows_ref[0:1, lanes], 1.0, 0.0)
-        before = jnp.dot(named.astype(BF16), earlier, preferred_element_type=F32) + carry
-        rank = jnp.sum(named * before, axis=0, keepdims=True)
-        carry = carry + jnp.sum(named, axis=1, keepdims=True)
-        placed = ranks == rank
-        weight = rows_ref[6:7, lanes]
-        first = weight.astype(BF16).astype(F32)
-        second = (weight - first).astype(BF16).astype(F32)
-        parts = [rows_ref[1 + m : 2 + m, lanes] for m in range(5)]
-        parts += [first, second, weight - first - second]
-        values = jnp.concatenate([jnp.where(placed, row, 0.0) for row in parts], axis=0)
-        table = table + lax.dot_general(
-            named.astype(BF16),
-            values.astype(BF16),
-            (((1,), (1,)), ((), ())),
-            preferred_element_type=F32,
-        )
+    for k in range(K):
+        for start in range(0, E, 256):
+            lanes = slice(start, start + 256)
+            named = jnp.where(devices == owner_ref[k : k + 1, lanes], 1.0, 0.0)
+            before = jnp.dot(named.astype(BF16), earlier, preferred_element_type=F32) + carry
+            rank = jnp.sum(named * before, axis=0, keepdims=True)
+            carry = carry + jnp.sum(named, axis=1, keepdims=True)
+            placed = ranks == rank
+            weight = weight_ref[k : k + 1, lanes]
+            first = weight.astype(BF16).astype(F32)
+            second = (weight - first).astype(BF16).astype(F32)
+            slot = slot_ref[k : k + 1, lanes]
+            element = lax.broadcasted_iota(jnp.int32, (1, 256), 1) + (start + 1)
+            parts = [
+                (element // 128).astype(F32),
+                lax.rem(element, 128).astype(F32),
+                jnp.full((1, 256), float(k), F32),
+                (slot // 128).astype(F32),
+                lax.rem(slot, 128).astype(F32),
+                first,
+                second,
+                weight - first - second,
+            ]
+            values = jnp.concatenate([jnp.where(placed, row, 0.0) for row in parts], axis=0)
+            table = table + lax.dot_general(
+                named.astype(BF16),
+                values.astype(BF16),
+                (((1,), (1,)), ((), ())),
+                preferred_element_type=F32,
+            )
     return table.astype(BF16)
 
 
@@ -99,10 +111,10 @@
 
 
 def kernel(
-    states_ref, v_ref, inverse_ref, own_ref, next_ref, project_ref, rows_ref, out0, out1, out2,
-    u_ref, g_ref, p_ref, lim_ref, sides, packed, means, mean_sides, mean_packed,
+    states_ref, v_ref, inverse_ref, own_ref, next_ref, project_ref,
+    owner_hbm, slot_hbm, weight_hbm, out0, out1, out2, owner_ref, slot_ref, weight_ref, u_ref, g_ref, p_ref, lim_ref, sides, packed, means, mean_sides, mean_packed,
     tb0, tb1, tb2, ar0, ar1, ar2, at0, at1, at2, bs0, bs1, bs2, br0, br1, br2,
-    cs0, cs1, cs2, cr0, cr1, cr2, ct0, ct1, ct2, split, picked, pair,
+    cs0, cs1, cs2, cr0, cr1, cr2, ct0, ct1, ct2, sp0, sp1, sp2, picked, pair,
     u_sem, h_send, h_recv, m_send, m_recv,
     a_send, a_recv, f_send, f_recv, t_send, t_recv, b_send, b_recv, c_send, c_recv, d_send, d_recv,
     own_sem,
@@ -136,7 +148,13 @@
         )
         for j in range(EX)
     ]
-    for load in loads:
+    lists = [
+        pltpu.make_async_copy(source, target, u_sem.at[EX + i])
+        for i, (source, target) in enumerate(
+            ((owner_hbm, owner_ref), (slot_hbm, slot_ref), (weight_hbm, weight_ref))
+        )
+    ]
+    for load in loads + lists:
         load.start()
     barrier = pltpu.get_barrier_semaphore()
     for device in partners:
@@ -270,7 +288,7 @@
         packed[1, rows, :] = high
         return 0
 
-    for load in loads:
+    for load in loads + lists:
         load.wait()
     lax.fori_loop(0, F, pack, 0)
     pl.semaphore_wait(barrier, len(partners))
@@ -373,16 +391,18 @@
                 rows = slice((first + f) * Q, (first + f + 1) * Q)
                 values = jnp.maximum(lim_ref[rows, block(j)], lower[f : f + 1])
                 lim_ref[rows, block(j)] = jnp.minimum(values, upper[f : f + 1])
-        for h in (0, 1):
-            states_copy(p, 1, h).start()
-            states_copy(p, 3, 1 - h).start()
+        states_copy(p, 1, 0).start()
+        states_copy(p, 3, 1).start()
 
     for p in range(3):
         edges(p)
     for p in range(3):
         limit(p)
 
-    table = rank_table(rows_ref)
+    table = rank_table(owner_ref, slot_ref, weight_ref)
+    for p in range(3):
+        states_copy(p, 1, 1).start()
+        states_copy(p, 3, 0).start()
     for p in range(3):
         axes = PARTS[p][2]
         part_table(table, axes, tables[p])
@@ -397,127 +417,120 @@
     element = lax.broadcasted_iota(jnp.int32, (E, 256), 0).astype(F32)
     quarter = lax.rem(lax.broadcasted_iota(jnp.int32, (1, 256), 1) // CAP, 4)
 
-    def route(p):
-        first, count, axes = PARTS[p]
+    split = (sp0, sp1, sp2)
+
+    def cut(p, d):
+        first, count, _ = PARTS[p]
         rows = count * Q
-        me_b = here[axes[1]]
-        for d in (0, 1, 3, 2):
-            if d:
-                table_copy(p, d).wait_recv()
-            if d == 2:
-                relay_copy(p, 1).wait_recv()
-                relay_copy(p, 3).wait_recv()
-            elif d:
-                states_copy(p, d, 1 - d // 2).wait_recv()
-            j = (4 - d) % 4
-            values = lim_ref[first * Q : first * Q + rows, :] if d == 0 else ar[p][3 - d]
-            high, low = halves(values)
-            split[j, 0:rows, :] = high
-            split[j, rows : 2 * rows, :] = low
-
-        def towards(step, _):
-            d = 3 - step
-            group = lax.rem(me_b + d, 4) * 2
-
-            def info_of(j, what):
-                tile = at[p][j, what]
-                lanes = []
-                for core in range(2):
-                    row = jnp.where(row8 == group + core, tile, 0.0)
-                    row = jnp.sum(row, axis=0, keepdims=True)
-                    lanes.append(pltpu.roll(row, CAP * j, 1) if j else row)
-                return jnp.concatenate(lanes, axis=1)
-
-            infos = []
-            for j in range(4):
-                infos.append([info_of(j, what) for what in (1, 2, 3)])
-                hot = jnp.where(element == info_of(j, 0), 1.0, 0.0).astype(BF16)
-                made = jnp.dot(split[j, 0 : 2 * rows, :], hot, preferred_element_type=F32)
-                picked[j, 0:rows, :] = made[0:rows] + made[rows:]
-            slots = jnp.zeros((8, 256), F32)
-            for o in range(4):
-                which, slot, weight = infos[3]
+        if d == 2:
+            relay_copy(p, 1).wait_recv()
+            relay_copy(p, 3).wait_recv()
+        elif d:
+            states_copy(p, d, 1 - d // 2).wait_recv()
+        values = lim_ref[first * Q : first * Q + rows, :] if d == 0 else ar[p][3 - d]
+        high, low = halves(values)
+        split[p][(4 - d) % 4, 0:rows, :] = high
+        split[p][(4 - d) % 4, rows : 2 * rows, :] = low
+
+    def route(p, d):
+        _, count, axes = PARTS[p]
+        rows = count * Q
+        group = lax.rem(here[axes[1]] + d, 4) * 2
+
+        def info_of(j, what):
+            tile = at[p][j, what]
+            lanes = []
+            for core in range(2):
+                row = jnp.where(row8 == group + core, tile, 0.0)
+                row = jnp.sum(row, axis=0, keepdims=True)
+                lanes.append(pltpu.roll(row, CAP * j, 1) if j else row)
+            return jnp.concatenate(lanes, axis=1)
+
+        infos = []
+        for j in range(4):
+            infos.append([info_of(j, what) for what in (1, 2, 3)])
+            hot = jnp.where(element == info_of(j, 0), 1.0, 0.0).astype(BF16)
+            made = jnp.dot(split[p][j], hot, preferred_element_type=F32)
+            picked[j, 0:rows, :] = made[0:rows] + made[rows:]
+        slots = jnp.zeros((8, 256), F32)
+        for o in range(4):
+            which, slot, weight = infos[3]
+            for j in range(3):
+                mine = quarter == (o + j) % 4
+                which = jnp.where(mine, infos[j][0], which)
+                slot = jnp.where(mine, infos[j][1], slot)
+                weight = jnp.where(mine, infos[j][2], weight)
+            for f in range(count):
+                part = slice(f * Q, (f + 1) * Q)
+                values = picked[3, part, :]
                 for j in range(3):
-                    mine = quarter == (o + j) % 4
-                    which = jnp.where(mine, infos[j][0], which)
-                    slot = jnp.where(mine, infos[j][1], slot)
-                    weight = jnp.where(mine, infos[j][2], weight)
-                for f in range(count):
-                    part = slice(f * Q, (f + 1) * Q)
-                    values = picked[3, part, :]
-                    for j in range(3):
-                        values = jnp.where(quarter == (o + j) % 4, picked[j, part, :], values)
-                    made = product(p_ref[...], values)
-                    chosen = made[3 * Q :]
-                    for k in range(3):
-                        chosen = jnp.where(which == float(k), made[k * Q : (k + 1) * Q], chosen)
-                    chosen = chosen * weight
-                    place = slice(o * rows + f * Q, o * rows + (f + 1) * Q)
-                    bs[p][d, 0, place, :] = chosen[:, 0:128]
-                    bs[p][d, 1, place, :] = chosen[:, 128:256]
-                slots = jnp.where(row256 == o, slot, slots)
-            bs[p][d, 0, 4 * rows : 4 * rows + 8, :] = slots[:, 0:128]
-            bs[p][d, 1, 4 * rows : 4 * rows + 8, :] = slots[:, 128:256]
-            block_copy(p, d, 1).start()
-
-            @pl.when(d > 0)
-            def _():
-                block_copy(p, d, 0).start()
-
-            return 0
-
-        lax.fori_loop(0, 4, towards, 0)
-        own_copy(p).start()
-
-    def gather(p):
+                    values = jnp.where(quarter == (o + j) % 4, picked[j, part, :], values)
+                made = product(p_ref[...], values)
+                chosen = made[3 * Q :]
+                for k in range(3):
+                    chosen = jnp.where(which == float(k), made[k * Q : (k + 1) * Q], chosen)
+                chosen = chosen * weight
+                place = slice(o * rows + f * Q, o * rows + (f + 1) * Q)
+                bs[p][d, 0, place, :] = chosen[:, 0:128]
+                bs[p][d, 1, place, :] = chosen[:, 128:256]
+            slots = jnp.where(row256 == o, slot, slots)
+        bs[p][d, 0, 4 * rows : 4 * rows + 8, :] = slots[:, 0:128]
+        bs[p][d, 1, 4 * rows : 4 * rows + 8, :] = slots[:, 128:256]
+        block_copy(p, d, 1).start()
+
+        @pl.when(d > 0)
+        def _():
+            block_copy(p, d, 0).start()
+
+
+    def gather(p, number):
         _, count, axes = PARTS[p]
         rows = count * Q
         me_c = here[axes[2]]
-        for number, d in enumerate((0, 1, 3, 2)):
-            if d == 0:
-                own_copy(p).wait()
-                block_copy(p, 0, 1).wait_recv()
-            else:
-                block_copy(p, d, 0).wait_recv()
-                block_copy(p, d, 1).wait_recv()
-            slot_of = (4 - d) % 4
-
-            def owner(distance, number=number, slot_of=slot_of):
-                o = lax.rem(me_c + distance, 4)
-                place = pl.ds(pl.multiple_of(o * rows, rows), rows)
-                high, low = halves(br[p][slot_of, place, :])
-                pair[0:rows, :] = high
-                pair[rows : 2 * rows, :] = low
-                slot = br[p][slot_of, 4 * rows : 4 * rows + 8, :]
-                slot = jnp.sum(jnp.where(row256 == o, slot, 0.0), axis=0, keepdims=True)
-                hot = jnp.where(element == slot, 1.0, 0.0)
-                made = lax.dot_general(
-                    pair[0 : 2 * rows, :],
-                    hot.astype(BF16),
-                    (((1,), (1,)), ((), ())),
-                    preferred_element_type=F32,
-                )
-                total = made[0:rows] + made[rows:]
-                if number > 0:
-                    total = total + cs[p][o]
-                cs[p][o] = total
-
-            if number < 3:
-
-                def step(distance, _, owner=owner):
-                    owner(distance)
-                    return 0
-
-                lax.fori_loop(0, 4, step, 0)
-            else:
-                owner(2)
-                far_sum(p, 1).start()
-                far_sum(p, 3).start()
-                owner(1)
-                near_sum(p, 1, 1).start()
-                owner(3)
-                near_sum(p, 3, 0).start()
-                owner(0)
+        d = (0, 1, 3, 2)[number]
+        if d == 0:
+            own_copy(p).wait()
+        else:
+            block_copy(p, d, 0).wait_recv()
+        block_copy(p, d, 1).wait_recv()
+        slot_of = (4 - d) % 4
+
+        def owner(distance):
+            o = lax.rem(me_c + distance, 4)
+            place = pl.ds(pl.multiple_of(o * rows, rows), rows)
+            high, low = halves(br[p][slot_of, place, :])
+            pair[0:rows, :] = high
+            pair[rows : 2 * rows, :] = low
+            slot = br[p][slot_of, 4 * rows : 4 * rows + 8, :]
+            slot = jnp.sum(jnp.where(row256 == o, slot, 0.0), axis=0, keepdims=True)
+            hot = jnp.where(element == slot, 1.0, 0.0)
+            made = lax.dot_general(
+                pair[0 : 2 * rows, :],
+                hot.astype(BF16),
+                (((1,), (1,)), ((), ())),
+                preferred_element_type=F32,
+            )
+            total = made[0:rows] + made[rows:]
+            if number > 0:
+                total = total + cs[p][o]
+            cs[p][o] = total
+
+        if number < 3:
+
+            def step(distance, _):
+                owner(distance)
+                return 0
+
+            lax.fori_loop(0, 4, step, 0)
+        else:
+            owner(2)
+            far_sum(p, 1).start()
+            far_sum(p, 3).start()
+            owner(1)
+            near_sum(p, 1, 1).start()
+            owner(3)
+            near_sum(p, 3, 0).start()
+            owner(0)
 
     def combine(p):
         half = PARTS[p][1] * Q // 2
@@ -536,12 +549,32 @@
             total = total + cr[p][d // 2]
         out[p][...] = total
 
-    for p in range(3):
-        route(p)
-    gather(2)
+    for d in (0, 1, 3):
+        for p in range(3):
+            cut(p, d)
+    for p in range(3):
+        cut(p, 2)
+        for d in (1, 2, 3):
+            table_copy(p, d).wait_recv()
+
+    def towards(step, _):
+        d = lax.rem(6 - step + (step // 2) * (2 * step - 1), 4)
+        for p in range(3):
+            route(p, d)
+        return 0
+
+    lax.fori_loop(0, 4, towards, 0)
+    for p in range(3):
+        own_copy(p).start()
+    for number in range(4):
+        gather(2, number)
+        if number == 0:
+            gather(0, 0)
+            gather(1, 0)
     combine(2)
-    gather(0)
-    gather(1)
+    for number in range(1, 4):
+        gather(0, number)
+        gather(1, number)
     for p in (0, 1):
         combine(p)
     for p in (2, 0, 1):
@@ -574,31 +607,17 @@
     new_slot,
     intersection_weight,
 ):
-    owner = new_owner.reshape(E, K).T.reshape(E * K)
-    slot = new_slot.reshape(E, K).T.reshape(E * K)
-    weight = intersection_weight.reshape(E, K).T.reshape(E * K)
-    which = jnp.arange(E * K, dtype=jnp.int32)
-    element = which % E + 1
-    listing = jnp.stack(
-        [
-            owner.astype(F32),
-            (element // 128).astype(F32),
-            (element % 128).astype(F32),
-            (which // E).astype(F32),
-            (slot // 128).astype(F32),
-            (slot % 128).astype(F32),
-            weight,
-            jnp.zeros((E * K,), F32),
-        ]
-    )
     rows = [count * Q for _, count, _ in PARTS]
     dma = pltpu.SemaphoreType.DMA
     made = pl.pallas_call(
         kernel,
         out_shape=[jax.ShapeDtypeStruct((r, E), F32) for r in rows],
-        in_specs=[pl.BlockSpec(memory_space=pl.ANY)] + [VMEM] * 6,
+        in_specs=[pl.BlockSpec(memory_space=pl.ANY)] + [VMEM] * 5 + [HBM] * 3,
         out_specs=[VMEM] * 3,
         scratch_shapes=[
+            pltpu.VMEM((K, E), jnp.int32),
+            pltpu.VMEM((K, E), jnp.int32),
+            pltpu.VMEM((K, E), F32),
             pltpu.VMEM((COLS, E), F32),
             pltpu.VMEM((8 * Q, 3 * Q), BF16),
             pltpu.VMEM((4 * Q, 3 * Q), BF16),
@@ -618,10 +637,10 @@
         + [pltpu.VMEM((2, r, E), F32) for r in rows]
         + [pltpu.VMEM((2, r // 2, E), F32) for r in rows]
         + [
-            pltpu.VMEM((4, 2 * max(rows), E), BF16),
+            *[pltpu.VMEM((4, 2 * r, E), BF16) for r in rows],
             pltpu.VMEM((4, max(rows), 256), F32),
             pltpu.VMEM((2 * max(rows), 256), BF16),
-            dma((4,)),
+            dma((EX + 3,)),
             *[dma((3, 4))] * 4,
             *[dma((3, 2, 2))] * 2,
             *[dma((3, 2))] * 2,
@@ -641,7 +660,9 @@
         flux_own,
         flux_next,
         projection,
-        listing,
+        new_owner.reshape(E, K).T,
+        new_slot.reshape(E, K).T,
+        intersection_weight.reshape(E, K).T,
     )
     return jnp.concatenate(made, axis=0).reshape(F, Q, E)
 

time: 109 us -> 101 us (0.927)
  the two profiles are of different devices: /device:TPU:106 before, /device:TPU:0 now
where the time goes in v4:
time: 101 us; the launch traced here: 100 us
  Pallas kernels  98.2 us (97%)
  other arithmetic  2.23 us (2%)
    pallas_call x1, Pallas kernels, body(): pl.pallas_call(kernel, out_shape=[jax.ShapeDtypeStruct((r, E), F32) for r...  98.2 us
    concatenate x1, other arithmetic, body(): return jnp.concatenate(made, axis=0).reshape(F, Q, E)  2.23 us

profile of v4, /device:TPU:0, one launch (start us, length us, event | category | flops | bytes accessed | tf_op | source)
XLA Modules:
  0.0 100.5 jit_solution(12347234896051318731)
XLA Ops:
  0.0 98.2 %shard_map.91 = (f32[192,512]{1,0:T(8,128)}, f32[192,512]{1,0:T(8,128)}, f32[128,512]{1,0:T(8,128)}) custom-call(f32[512,4,128]{2,1,0:T(4,128)} %bitcast.11, f32[4,4,128]{2,1,0:T(4,128)} %v_ref.1, f32[64,64]{1,0:T(8,128)} %inverse_ref.1, f32[4,64,64]{2,1,0:T(8,128)} %own_ref.1, f32[4,64,64]{2,1,0:T(8,128)} %next_ref.1, f32[4,64,64]{2,1,0:T(8,128)} %project_ref.1, ...), custom_call_target="tpu_custom_call" | custom-call | tf_op jit(solution)/shard_map/pallas_call | solution.py:612
  98.2 2.2 %pad_maximum_fusion = f32[512,512]{1,0:T(8,128)} fusion(f32[128,512]{1,0:T(8,128)} %get-tuple-element.10, f32[192,512]{1,0:T(8,128)} %get-tuple-element.9, f32[192,512]{1,0:T(8,128)} %get-tuple-element.8), kind=kLoop, calls=%fused_computation | loop fusion | flops 524288 | bytes 2097152 | tf_op jit(solution)/shard_map/concatenate | solution.py:667

commit v5 on v4

--- a/solution.py
+++ b/solution.py
@@ -141,7 +141,7 @@
         return (at_["z"] * 4 + at_["y"], at_["x"] * 2 + at_["c"])
 
     partners = [away(axis, d, core) for axis in "xyz" for d in (1, 2, 3) for core in (0, 1)]
-    partners += [away("x", 0, 1), *near]
+    partners += [away("x", 0, 1), *near[:2]]
     loads = [
         pltpu.make_async_copy(
             states_ref.at[:, j, :], u_ref.at[:, pl.ds(j * EY, EY)], u_sem.at[j]
@@ -291,12 +291,12 @@
     for load in loads + lists:
         load.wait()
     lax.fori_loop(0, F, pack, 0)
+    fold(inverse_ref, [own_ref[s] for s in range(4)] + [next_ref[s] for s in range(4)], g_ref)
+    fold(inverse_ref, [project_ref[k] for k in range(4)], p_ref)
     pl.semaphore_wait(barrier, len(partners))
     for p in range(3):
         for s in range(4):
             side_copy(p, s).start()
-    fold(inverse_ref, [own_ref[s] for s in range(4)] + [next_ref[s] for s in range(4)], g_ref)
-    fold(inverse_ref, [project_ref[k] for k in range(4)], p_ref)
 
     def interior(f, _):
         rows = pl.ds(pl.multiple_of(f * Q, Q), Q)
@@ -483,54 +483,58 @@
             block_copy(p, d, 0).start()
 
 
-    def gather(p, number):
-        _, count, axes = PARTS[p]
-        rows = count * Q
-        me_c = here[axes[2]]
+    def landed(p, number):
         d = (0, 1, 3, 2)[number]
         if d == 0:
             own_copy(p).wait()
         else:
             block_copy(p, d, 0).wait_recv()
         block_copy(p, d, 1).wait_recv()
-        slot_of = (4 - d) % 4
-
-        def owner(distance):
-            o = lax.rem(me_c + distance, 4)
-            place = pl.ds(pl.multiple_of(o * rows, rows), rows)
-            high, low = halves(br[p][slot_of, place, :])
-            pair[0:rows, :] = high
-            pair[rows : 2 * rows, :] = low
-            slot = br[p][slot_of, 4 * rows : 4 * rows + 8, :]
-            slot = jnp.sum(jnp.where(row256 == o, slot, 0.0), axis=0, keepdims=True)
-            hot = jnp.where(element == slot, 1.0, 0.0)
-            made = lax.dot_general(
-                pair[0 : 2 * rows, :],
-                hot.astype(BF16),
-                (((1,), (1,)), ((), ())),
-                preferred_element_type=F32,
-            )
-            total = made[0:rows] + made[rows:]
-            if number > 0:
-                total = total + cs[p][o]
-            cs[p][o] = total
-
-        if number < 3:
-
-            def step(distance, _):
-                owner(distance)
-                return 0
-
-            lax.fori_loop(0, 4, step, 0)
-        else:
-            owner(2)
-            far_sum(p, 1).start()
-            far_sum(p, 3).start()
-            owner(1)
+
+    def arrived(p, number, distance):
+        _, count, axes = PARTS[p]
+        rows = count * Q
+        slot_of = (0, 3, 1, 2)[number]
+        o = lax.rem(here[axes[2]] + distance, 4)
+        place = pl.ds(pl.multiple_of(o * rows, rows), rows)
+        high, low = halves(br[p][slot_of, place, :])
+        pair[0:rows, :] = high
+        pair[rows : 2 * rows, :] = low
+        slot = br[p][slot_of, 4 * rows : 4 * rows + 8, :]
+        slot = jnp.sum(jnp.where(row256 == o, slot, 0.0), axis=0, keepdims=True)
+        hot = jnp.where(element == slot, 1.0, 0.0)
+        made = lax.dot_general(
+            pair[0 : 2 * rows, :],
+            hot.astype(BF16),
+            (((1,), (1,)), ((), ())),
+            preferred_element_type=F32,
+        )
+        total = made[0:rows] + made[rows:]
+        if number > 0:
+            total = total + cs[p][o]
+        cs[p][o] = total
+
+    def gather(p, number):
+        landed(p, number)
+
+        def step(distance, _):
+            arrived(p, number, distance)
+            return 0
+
+        lax.fori_loop(0, 4, step, 0)
+
+    def gather_last(ps):
+        for distance in (2, 1, 3, 0):
+            for p in ps:
+                if distance == 2:
+                    landed(p, 3)
+                arrived(p, 3, distance)
+                if distance == 2:
+                    far_sum(p, 1).start()
+                    far_sum(p, 3).start()
+        for p in ps:
             near_sum(p, 1, 1).start()
-            owner(3)
             near_sum(p, 3, 0).start()
-            owner(0)
 
     def combine(p):
         half = PARTS[p][1] * Q // 2
@@ -542,12 +546,10 @@
             near_sum(p, d, d // 2).start()
 
     def finish(p):
-        total = cs[p][here[PARTS[p][2][2]]]
-        for d in (1, 3):
-            for h in (0, 1):
-                near_sum(p, d, h).wait_recv()
-            total = total + cr[p][d // 2]
-        out[p][...] = total
+        for h in (0, 1):
+            near_sum(p, 1, h).wait_recv()
+            near_sum(p, 3, h).wait_recv()
+        out[p][...] = cs[p][owner_at(p, 0)] + cr[p][0] + cr[p][1]
 
     for d in (0, 1, 3):
         for p in range(3):
@@ -566,18 +568,17 @@
     lax.fori_loop(0, 4, towards, 0)
     for p in range(3):
         own_copy(p).start()
-    for number in range(4):
-        gather(2, number)
-        if number == 0:
-            gather(0, 0)
-            gather(1, 0)
-    combine(2)
-    for number in range(1, 4):
+    for p in (2, 0, 1):
+        gather(p, 0)
+    gather(2, 1)
+    gather(2, 2)
+    for number in (1, 2):
         gather(0, number)
         gather(1, number)
-    for p in (0, 1):
+    gather_last((0, 1, 2))
+    for p in (0, 1, 2):
         combine(p)
-    for p in (2, 0, 1):
+    for p in (0, 1, 2):
         finish(p)
     for p in range(3):
         for s in range(4):

time: 101 us -> 98.2 us (0.972)
  Pallas kernels: 98.2 us -> 95.4 us
    pallas_call x1, Pallas kernels: 98.2 us -> 95.4 us  [body(): pl.pallas_call(kernel, out_shape=[jax.ShapeDtypeStruct((r, E), F32) for r...]
where the time goes in v5:
time: 98.2 us; the launch traced here: 97.6 us
  Pallas kernels  95.4 us (97%)
  other arithmetic  2.23 us (2%)
    pallas_call x1, Pallas kernels, body(): pl.pallas_call(kernel, out_shape=[jax.ShapeDtypeStruct((r, E), F32) for r...  95.4 us
    concatenate x1, other arithmetic, body(): return jnp.concatenate(made, axis=0).reshape(F, Q, E)  2.23 us

profile of v5, /device:TPU:0, one launch (start us, length us, event | category | flops | bytes accessed | tf_op | source)
XLA Modules:
  0.0 97.6 jit_solution(9237079376659316564)
XLA Ops:
  0.0 95.4 %shard_map.91 = (f32[192,512]{1,0:T(8,128)}, f32[192,512]{1,0:T(8,128)}, f32[128,512]{1,0:T(8,128)}) custom-call(f32[512,4,128]{2,1,0:T(4,128)} %bitcast.11, f32[4,4,128]{2,1,0:T(4,128)} %v_ref.1, f32[64,64]{1,0:T(8,128)} %inverse_ref.1, f32[4,64,64]{2,1,0:T(8,128)} %own_ref.1, f32[4,64,64]{2,1,0:T(8,128)} %next_ref.1, f32[4,64,64]{2,1,0:T(8,128)} %project_ref.1, ...), custom_call_target="tpu_custom_call" | custom-call | tf_op jit(solution)/shard_map/pallas_call | solution.py:613
  95.4 2.2 %pad_maximum_fusion = f32[512,512]{1,0:T(8,128)} fusion(f32[128,512]{1,0:T(8,128)} %get-tuple-element.10, f32[192,512]{1,0:T(8,128)} %get-tuple-element.9, f32[192,512]{1,0:T(8,128)} %get-tuple-element.8), kind=kLoop, calls=%fused_computation | loop fusion | flops 524288 | bytes 2097152 | tf_op jit(solution)/shard_map/concatenate | solution.py:668

commit v6 on v5

--- a/solution.py
+++ b/solution.py
@@ -114,7 +114,7 @@
     states_ref, v_ref, inverse_ref, own_ref, next_ref, project_ref,
     owner_hbm, slot_hbm, weight_hbm, out0, out1, out2, owner_ref, slot_ref, weight_ref, u_ref, g_ref, p_ref, lim_ref, sides, packed, means, mean_sides, mean_packed,
     tb0, tb1, tb2, ar0, ar1, ar2, at0, at1, at2, bs0, bs1, bs2, br0, br1, br2,
-    cs0, cs1, cs2, cr0, cr1, cr2, ct0, ct1, ct2, sp0, sp1, sp2, picked, pair,
+    cs0, cs1, cs2, cr0, cr1, cr2, ct0, ct1, ct2, sp0, sp1, sp2, pk0, pk1, pk2, pair,
     u_sem, h_send, h_recv, m_send, m_recv,
     a_send, a_recv, f_send, f_recv, t_send, t_recv, b_send, b_recv, c_send, c_recv, d_send, d_recv,
     own_sem,
@@ -417,7 +417,7 @@
     element = lax.broadcasted_iota(jnp.int32, (E, 256), 0).astype(F32)
     quarter = lax.rem(lax.broadcasted_iota(jnp.int32, (1, 256), 1) // CAP, 4)
 
-    split = (sp0, sp1, sp2)
+    split, picked = (sp0, sp1, sp2), (pk0, pk1, pk2)
 
     def cut(p, d):
         first, count, _ = PARTS[p]
@@ -432,26 +432,26 @@
         split[p][(4 - d) % 4, 0:rows, :] = high
         split[p][(4 - d) % 4, rows : 2 * rows, :] = low
 
+    def info_of(p, d, j, what):
+        group = lax.rem(here[PARTS[p][2][1]] + d, 4) * 2
+        tile = at[p][j, what]
+        lanes = []
+        for core in range(2):
+            row = jnp.where(row8 == group + core, tile, 0.0)
+            row = jnp.sum(row, axis=0, keepdims=True)
+            lanes.append(pltpu.roll(row, CAP * j, 1) if j else row)
+        return jnp.concatenate(lanes, axis=1)
+
+    def pick(p, d, j):
+        rows = PARTS[p][1] * Q
+        hot = jnp.where(element == info_of(p, d, j, 0), 1.0, 0.0).astype(BF16)
+        made = jnp.dot(split[p][j], hot, preferred_element_type=F32)
+        picked[p][j] = made[0:rows] + made[rows:]
+
     def route(p, d):
         _, count, axes = PARTS[p]
         rows = count * Q
-        group = lax.rem(here[axes[1]] + d, 4) * 2
-
-        def info_of(j, what):
-            tile = at[p][j, what]
-            lanes = []
-            for core in range(2):
-                row = jnp.where(row8 == group + core, tile, 0.0)
-                row = jnp.sum(row, axis=0, keepdims=True)
-                lanes.append(pltpu.roll(row, CAP * j, 1) if j else row)
-            return jnp.concatenate(lanes, axis=1)
-
-        infos = []
-        for j in range(4):
-            infos.append([info_of(j, what) for what in (1, 2, 3)])
-            hot = jnp.where(element == info_of(j, 0), 1.0, 0.0).astype(BF16)
-            made = jnp.dot(split[p][j], hot, preferred_element_type=F32)
-            picked[j, 0:rows, :] = made[0:rows] + made[rows:]
+        infos = [[info_of(p, d, j, what) for what in (1, 2, 3)] for j in range(4)]
         slots = jnp.zeros((8, 256), F32)
         for o in range(4):
             which, slot, weight = infos[3]
@@ -462,9 +462,9 @@
                 weight = jnp.where(mine, infos[j][2], weight)
             for f in range(count):
                 part = slice(f * Q, (f + 1) * Q)
-                values = picked[3, part, :]
+                values = picked[p][3, part, :]
                 for j in range(3):
-                    values = jnp.where(quarter == (o + j) % 4, picked[j, part, :], values)
+                    values = jnp.where(quarter == (o + j) % 4, picked[p][j, part, :], values)
                 made = product(p_ref[...], values)
                 chosen = made[3 * Q :]
                 for k in range(3):
@@ -478,9 +478,13 @@
         bs[p][d, 1, 4 * rows : 4 * rows + 8, :] = slots[:, 128:256]
         block_copy(p, d, 1).start()
 
-        @pl.when(d > 0)
-        def _():
+        if isinstance(d, int):
             block_copy(p, d, 0).start()
+        else:
+
+            @pl.when(d > 0)
+            def _():
+                block_copy(p, d, 0).start()
 
 
     def landed(p, number):
@@ -555,17 +559,25 @@
         for p in range(3):
             cut(p, d)
     for p in range(3):
-        cut(p, 2)
         for d in (1, 2, 3):
             table_copy(p, d).wait_recv()
+    for p in range(3):
+        for j in (0, 1, 3):
+            pick(p, 2, j)
+    for p in range(3):
+        cut(p, 2)
+        pick(p, 2, 2)
+        route(p, 2)
 
     def towards(step, _):
         d = lax.rem(6 - step + (step // 2) * (2 * step - 1), 4)
         for p in range(3):
+            for j in range(4):
+                pick(p, d, j)
             route(p, d)
         return 0
 
-    lax.fori_loop(0, 4, towards, 0)
+    lax.fori_loop(1, 4, towards, 0)
     for p in range(3):
         own_copy(p).start()
     for p in (2, 0, 1):
@@ -639,7 +651,7 @@
         + [pltpu.VMEM((2, r // 2, E), F32) for r in rows]
         + [
             *[pltpu.VMEM((4, 2 * r, E), BF16) for r in rows],
-            pltpu.VMEM((4, max(rows), 256), F32),
+            *[pltpu.VMEM((4, r, 256), F32) for r in rows],
             pltpu.VMEM((2 * max(rows), 256), BF16),
             dma((EX + 3,)),
             *[dma((3, 4))] * 4,

time: 98.2 us -> 97.3 us (level)
  Pallas kernels: 95.4 us -> 93.8 us
    pallas_call x1, Pallas kernels: 95.4 us -> 93.8 us  [body(): pl.pallas_call(kernel, out_shape=[jax.ShapeDtypeStruct((r, E), F32) for r...]
where the time goes in v6:
time: 97.3 us; the launch traced here: 96 us
  Pallas kernels  93.8 us (96%)
  other arithmetic  2.23 us (2%)
    pallas_call x1, Pallas kernels, body(): pl.pallas_call(kernel, out_shape=[jax.ShapeDtypeStruct((r, E), F32) for r...  93.8 us
    concatenate x1, other arithmetic, body(): return jnp.concatenate(made, axis=0).reshape(F, Q, E)  2.23 us

profile of v6, /device:TPU:0, one launch (start us, length us, event | category | flops | bytes accessed | tf_op | source)
XLA Modules:
  0.0 96.0 jit_solution(15541471766839036921)
XLA Ops:
  0.0 93.8 %shard_map.91 = (f32[192,512]{1,0:T(8,128)}, f32[192,512]{1,0:T(8,128)}, f32[128,512]{1,0:T(8,128)}) custom-call(f32[512,4,128]{2,1,0:T(4,128)} %bitcast.11, f32[4,4,128]{2,1,0:T(4,128)} %v_ref.1, f32[64,64]{1,0:T(8,128)} %inverse_ref.1, f32[4,64,64]{2,1,0:T(8,128)} %own_ref.1, f32[4,64,64]{2,1,0:T(8,128)} %next_ref.1, f32[4,64,64]{2,1,0:T(8,128)} %project_ref.1, ...), custom_call_target="tpu_custom_call" | custom-call | tf_op jit(solution)/shard_map/pallas_call | solution.py:625
  93.8 2.2 %pad_maximum_fusion = f32[512,512]{1,0:T(8,128)} fusion(f32[128,512]{1,0:T(8,128)} %get-tuple-element.10, f32[192,512]{1,0:T(8,128)} %get-tuple-element.9, f32[192,512]{1,0:T(8,128)} %get-tuple-element.8), kind=kLoop, calls=%fused_computation | loop fusion | flops 524288 | bytes 2097152 | tf_op jit(solution)/shard_map/concatenate | solution.py:680

commit v7 on v6

--- a/solution.py
+++ b/solution.py
@@ -292,7 +292,6 @@
         load.wait()
     lax.fori_loop(0, F, pack, 0)
     fold(inverse_ref, [own_ref[s] for s in range(4)] + [next_ref[s] for s in range(4)], g_ref)
-    fold(inverse_ref, [project_ref[k] for k in range(4)], p_ref)
     pl.semaphore_wait(barrier, len(partners))
     for p in range(3):
         for s in range(4):
@@ -399,10 +398,11 @@
     for p in range(3):
         limit(p)
 
-    table = rank_table(owner_ref, slot_ref, weight_ref)
+    fold(inverse_ref, [project_ref[k] for k in range(4)], p_ref)
     for p in range(3):
         states_copy(p, 1, 1).start()
         states_copy(p, 3, 0).start()
+    table = rank_table(owner_ref, slot_ref, weight_ref)
     for p in range(3):
         axes = PARTS[p][2]
         part_table(table, axes, tables[p])

time: 97.3 us -> 97.5 us (level)
  no operation moved by 1% of the time
where the time goes in v7:
time: 97.5 us; the launch traced here: 95.9 us
  Pallas kernels  93.7 us (96%)
  other arithmetic  2.23 us (2%)
    pallas_call x1, Pallas kernels, body(): pl.pallas_call(kernel, out_shape=[jax.ShapeDtypeStruct((r, E), F32) for r...  93.7 us
    concatenate x1, other arithmetic, body(): return jnp.concatenate(made, axis=0).reshape(F, Q, E)  2.23 us

profile of v7, /device:TPU:0, one launch (start us, length us, event | category | flops | bytes accessed | tf_op | source)
XLA Modules:
  0.0 95.9 jit_solution(2960846866092530861)
XLA Ops:
  0.0 93.7 %shard_map.91 = (f32[192,512]{1,0:T(8,128)}, f32[192,512]{1,0:T(8,128)}, f32[128,512]{1,0:T(8,128)}) custom-call(f32[512,4,128]{2,1,0:T(4,128)} %bitcast.11, f32[4,4,128]{2,1,0:T(4,128)} %v_ref.1, f32[64,64]{1,0:T(8,128)} %inverse_ref.1, f32[4,64,64]{2,1,0:T(8,128)} %own_ref.1, f32[4,64,64]{2,1,0:T(8,128)} %next_ref.1, f32[4,64,64]{2,1,0:T(8,128)} %project_ref.1, ...), custom_call_target="tpu_custom_call" | custom-call | tf_op jit(solution)/shard_map/pallas_call | solution.py:625
  93.7 2.2 %pad_maximum_fusion = f32[512,512]{1,0:T(8,128)} fusion(f32[128,512]{1,0:T(8,128)} %get-tuple-element.10, f32[192,512]{1,0:T(8,128)} %get-tuple-element.9, f32[192,512]{1,0:T(8,128)} %get-tuple-element.8), kind=kLoop, calls=%fused_computation | loop fusion | flops 524288 | bytes 2097152 | tf_op jit(solution)/shard_map/concatenate | solution.py:680
